TPU v7x, 128 devices: a whole 4x4x4 slice. The times are simulated.
128 devices in a mesh: ao: 16 (over z, x), aux: 8 (over y, core).
Axes of the slice: x: 4, y: 4, z: 4, core: 2. Of those that a mesh axis runs over, the one named last changes fastest.
Arguments:
- integrals: bfloat16 [16, 8, 8, 128, 16, 128], P('ao', 'aux'), may hold values from -0.25 to 0.25
- block_list: int32 [16, 16, 2], P('ao'), may hold values from 0 to 7, as said below
- pair_count: int32 [16, 16], P('ao'), may hold values from 0 to 2, as said below
- occupied: bfloat16 [16, 8, 16, 2, 128, 128], P('ao'), may hold values from -0.125 to 0.125
- virtual: bfloat16 [8, 128, 128], P('aux'), may hold values from -0.5 to 0.5
Outputs:
- response: float32 [16, 16], P('ao', 'aux')
Inputs may be any that keep to these rules, and one draw needn't show every extreme that they name: For every i and d the 2 entries block_list[i,d,:] are different. pair_count[i,i] = 2 for every i.
All inputs are finite; a program needn't handle non-finite values.
Results may differ from a plain program's by a relative error of at most 0.0042.
Values may be sent and summed in bfloat16 or wider, within the bound.
No kernel may reach another device: no remote copies, remote signals or barrier semaphores. Data moves between devices by JAX's collectives and lax.ppermute only.
A program may use at most 128 MiB of HBM per device.

v0:
```python
import functools

import jax
import jax.numpy as jnp
from jax import lax
from jax.experimental import pallas as pl
from jax.experimental.pallas import tpu as pltpu
from jax.sharding import PartitionSpec as P

BS = 128
NB = 8
AB = 16
WIDE = AB * BS
ROWS = NB * BS
AXES = ("ao", "aux")
SIDE = 4
N_AO = 16
LIST = 48
CHUNKS = 2
PER = NB // CHUNKS
G = 3
ALWAYS = 4
STEPS = 6
DELAY = 2
RELAY = 32
FIRST = G
FAR = 2
ORDER = (0, 1, 3, FAR)
PARTS = 4
SEND, TAKE, NEAR = 16, 64, 128
VMEM_BYTES = 56 * 1024 * 1024


def shift(ring, step):
    pairs = []
    for z in range(SIDE):
        for x in range(SIDE):
            for aux in range(8):
                along_x = (aux % 2 == 0) != ring
                to = z * SIDE + (x + step) % SIDE if along_x else (z + step) % SIDE * SIDE + x
                pairs.append(((z * SIDE + x) * 8 + aux, to * 8 + aux))
    return pairs


def across(array, step):
    return lax.ppermute(array, AXES, shift(False, step))


def around(array, step):
    return lax.ppermute(array, AXES, shift(True, step))


def index_of(core, t, e):
    return jnp.where(core == 0, t * SIDE + e, e * SIDE + t)


def pick(values, t):
    out = values[0]
    for s in range(1, SIDE):
        out = jnp.where(t == s, values[s], out)
    return out


def ring_plan(lists, core, e):
    def count(ts, td):
        td = index_of(core, td % SIDE, e)
        near = lists[index_of(core, ts, (e + ORDER[0]) % SIDE), 32 + td]
        for rel in ORDER[1:-1]:
            near = near + lists[index_of(core, ts, (e + rel) % SIDE), 32 + td]
        return near, near + lists[index_of(core, ts, (e + FAR) % SIDE), 32 + td]

    ones = [[count(t, t + step) for t in range(SIDE)] for step in (1, 3)]
    twos = [count(t, t + 2) for t in range(SIDE)]

    def layout(ups):
        ways = []
        for way, sender in ((0, 3), (1, 1)):
            two, two_near, gap, early, late, own, held_up = [], [], [], [], [], [], []
            for t in range(SIDE):
                if way == 0:
                    h = ups[t]
                    hn = jnp.minimum(h, twos[t][0])
                else:
                    h = twos[t][1] - ups[t]
                    hn = jnp.maximum(twos[t][0] - ups[t], 0)
                u = jnp.maximum(FIRST - hn, 0)
                us = jnp.minimum(u, ones[way][t][0])
                two.append(h)
                two_near.append(hn)
                gap.append(u)
                early.append(us)
                late.append(u + h)
                own.append(u + h + ones[way][t][1] - us)
                held_up.append(DELAY * G + jnp.where(h > hn, u, 0))
            relay = [jnp.maximum(own[t], held_up[(t + sender) % SIDE]) for t in range(SIDE)]
            length = [relay[t] + two[(t + sender) % SIDE] for t in range(SIDE)]
            ways.append(dict(two=two, two_near=two_near, gap=gap, early=early, late=late, relay=relay, length=length))
        return ways

    def longest(ups):
        up, down = layout(ups)
        return functools.reduce(jnp.maximum, up["length"] + down["length"])

    plain = [twos[t][1] // 2 for t in range(SIDE)]
    ups = list(plain)
    for _ in range(2):
        for t in range(SIDE):
            up, down = (way["length"] for way in layout(ups))
            excess = jnp.maximum(up[t], up[(t + 1) % SIDE]) - jnp.maximum(down[t], down[(t + 3) % SIDE])
            move = jnp.where(excess >= 0, excess // 2, -((-excess) // 2))
            ups[t] = jnp.clip(ups[t] - move, 0, twos[t][1])
    better = longest(ups) < longest(plain)
    ups = [jnp.where(better, a, b) for a, b in zip(ups, plain)]
    return ups, layout(ups), longest(ups)


def plan_kernel(came, where, table, lists):
    ao, aux = where[0], where[1]
    core = aux % 2
    z, x = ao // SIDE, ao % SIDE
    t = jnp.where(core == 0, z, x)
    e = jnp.where(core == 0, x, z)

    def place(r, _):
        i = index_of(core, (t - r // SIDE + SIDE) % SIDE, (e - r % SIDE + SIDE) % SIDE)
        for c in range(LIST):
            lists[i, c] = came[r, c]
        return 0

    lax.fori_loop(0, N_AO, place, 0)

    def ring(r, most):
        return jnp.maximum(most, ring_plan(lists, r // SIDE, r % SIDE)[2])

    table[0] = lax.fori_loop(0, 2 * SIDE, ring, jnp.int32(0))
    ups, ways, _ = ring_plan(lists, core, e)

    for r in range(G * STEPS):
        for way in range(2):
            table[SEND + 24 * way + r] = 0
            table[TAKE + 24 * way + r] = -1

    def each(ts, td, then):
        ts, td = ts % SIDE, td % SIDE
        d = index_of(core, td, e)
        n = jnp.int32(0)
        for rel in ORDER:
            i = index_of(core, ts, (e + rel) % SIDE)
            count = lists[i, 32 + d]
            for k in range(2):
                @pl.when(k < count)
                def _(n=n, i=i, k=k, rel=rel):
                    then(n, rel * NB + lists[i, 2 * d + k], 2 * i + k)
                n = n + jnp.where(k < count, 1, 0)
        return n

    def at_two(way, s, n):
        return n + jnp.where(n >= pick(way["two_near"], s), pick(way["gap"], s), 0)

    def at_one(way, s, n):
        early = pick(way["early"], s)
        return n + jnp.where(n < early, pick(way["two_near"], s), pick(way["late"], s) - early)

    my_up = pick(ups, t)

    def send_two(n, held, slot):
        @pl.when(n < my_up)
        def _():
            table[SEND + at_two(ways[0], t, n)] = held

        @pl.when(n >= my_up)
        def _():
            table[SEND + 24 + at_two(ways[1], t, n - my_up)] = held

    each(t, t + 2, send_two)
    opposite = (t + 2) % SIDE
    far_up = pick(ups, opposite)
    for way, step in ((0, 1), (1, 3)):
        sender = (t + 4 - step) % SIDE

        def send_one(n, held, slot, way=way):
            table[SEND + 24 * way + at_one(ways[way], t, n)] = held

        each(t, t + step, send_one)

        def relay(j, _, way=way, sender=sender):
            table[SEND + 24 * way + pick(ways[way]["relay"], t) + j] = RELAY + at_two(ways[way], sender, j)
            return 0

        lax.fori_loop(0, pick(ways[way]["two"], sender), relay, 0)

        def take_one(n, held, slot, way=way, sender=sender):
            table[TAKE + 24 * way + at_one(ways[way], sender, n)] = slot

        each(sender, t, take_one)

    def take_two(n, held, slot):
        @pl.when(n < far_up)
        def _():
            table[TAKE + pick(ways[0]["relay"], (t + 3) % SIDE) + n] = slot

        @pl.when(n >= far_up)
        def _():
            table[TAKE + 24 + pick(ways[1]["relay"], (t + 1) % SIDE) + n - far_up] = slot

    each(opposite, t, take_two)

    def near(n, held, slot):
        table[NEAR + n] = held * 32 + slot

    table[1] = each(t, t, near)


def plan(lists, where):
    smem = pl.BlockSpec(memory_space=pltpu.SMEM)
    return pl.pallas_call(
        plan_kernel,
        out_shape=jax.ShapeDtypeStruct((256,), jnp.int32),
        in_specs=[smem, smem],
        out_specs=smem,
        scratch_shapes=[pltpu.SMEM((N_AO, LIST), jnp.int32)],
    )(lists, where)


def pack_kernel(step, held, relays, table, *refs):
    refs = list(refs)
    tiles = {m: [refs.pop(0) for _ in range(CHUNKS)] for m in held}
    came = [refs.pop(0) for _ in range(2 * relays)]
    up, down, sems = refs
    waits = []
    for way, out in enumerate((up, down)):
        for h in range(G):
            code = table[SEND + 24 * way + G * step + h]
            dst = out.at[h]
            sem = sems.at[G * way + h]
            for m in held:
                for c, tile in enumerate(tiles[m]):
                    @pl.when(code // PER == m * CHUNKS + c)
                    def _(tile=tile, dst=dst, sem=sem, code=code):
                        pltpu.make_async_copy(tile.at[code % PER], dst, sem).start()
            for q in range(relays):
                for g in range(G):
                    @pl.when(code == RELAY + G * q + g)
                    def _(q=q, g=g, way=way, dst=dst, sem=sem):
                        pltpu.make_async_copy(came[2 * q + way].at[g], dst, sem).start()
            waits.append(pltpu.make_async_copy(tiles[0][0].at[0], dst, sem))
    for copy in waits:
        copy.wait()


def pack(step, table, tiles, came):
    relays = max(step - DELAY + 1, 0)
    held = [m for m in ORDER if G * step >= FIRST or m != FAR]
    smem = pl.BlockSpec(memory_space=pltpu.SMEM)
    vmem = pl.BlockSpec(memory_space=pltpu.VMEM)
    hbm = pl.BlockSpec(memory_space=pl.ANY)
    operands = [chunk for m in held for chunk in tiles[m]]
    for q in range(relays):
        operands += came[q]
    shape = jax.ShapeDtypeStruct((G, BS, WIDE), jnp.bfloat16)
    return pl.pallas_call(
        functools.partial(pack_kernel, step, held, relays),
        out_shape=[shape, shape],
        in_specs=[smem] + [hbm] * len(operands),
        out_specs=[vmem, vmem],
        scratch_shapes=[pltpu.SemaphoreType.DMA((2 * G,))],
        cost_estimate=pl.CostEstimate(flops=0, bytes_accessed=1024, transcendentals=0),
    )(table, *operands)


def gather(own_c, left, right, sems, wanted):
    n = jnp.int32(0)
    for ok, slot, start in wanted:
        @pl.when(ok)
        def _(n=n, slot=slot, start=start):
            at = pl.ds(pl.multiple_of(n * BS, BS), BS)
            pltpu.make_async_copy(own_c.at[:, slot // 2, slot % 2], left.at[:, :, at], sems.at[0]).start()
            start(right.at[at], sems.at[1])
        n = n + jnp.where(ok, 1, 0)
    return n


def arrive(own_c, left, right, sems, n):
    def one(_, carry):
        at = pl.ds(0, BS)
        pltpu.make_async_copy(own_c.at[:, 0, 0], left.at[:, :, at], sems.at[0]).wait()
        pltpu.make_async_copy(right.at[at], right.at[at], sems.at[1]).wait()
        return carry

    lax.fori_loop(0, n, one, 0)

    @pl.when(n % 2 == 1)
    def _():
        at = pl.ds(pl.multiple_of(n * BS, BS), BS)
        left[:, :, at] = jnp.zeros((NB, BS, BS), jnp.bfloat16)
        right[at, :] = jnp.zeros((BS, WIDE), jnp.bfloat16)


def contract(left, right, n, acc, cols):
    def pair(p, carry):
        at = pl.ds(pl.multiple_of(p * 2 * BS, 2 * BS), 2 * BS)
        acc[:, cols] += jnp.dot(
            left[:, :, at].reshape(ROWS, 2 * BS), right[at, cols], preferred_element_type=jnp.float32
        )
        return carry

    lax.fori_loop(0, (n + 1) // 2, pair, 0)


def from_steps(table, steps, came):
    wanted = []
    for q, step in enumerate(steps):
        for way in range(2):
            for h in range(G):
                slot = table[TAKE + 24 * way + G * step + h]

                def start(dst, sem, q=q, way=way, h=h):
                    pltpu.make_async_copy(came[2 * q + way].at[h], dst, sem).start()

                wanted.append((slot >= 0, jnp.maximum(slot, 0), start))
    return wanted


def sum_kernel(near, steps, clear, table, own_c, *refs):
    refs = list(refs)
    before = None if clear else refs.pop(0)
    tiles = {m: [refs.pop(0) for _ in range(CHUNKS)] for m in near}
    came = [refs.pop(0) for _ in range(2 * len(steps))]
    out, left, right, acc, sems = refs
    wanted = from_steps(table, steps, came)
    for s in range(2 * SIDE if near else 0):
        entry = table[NEAR + s]
        code = entry // 32
        here = jnp.bool_(False)
        for m in near:
            here = jnp.logical_or(here, code // NB == m)

        def start(dst, sem, code=code):
            for m in near:
                for c, chunk in enumerate(tiles[m]):
                    @pl.when(code // PER == m * CHUNKS + c)
                    def _():
                        pltpu.make_async_copy(chunk.at[code % PER], dst, sem).start()

        wanted.append((jnp.logical_and(s < table[1], here), entry % 32, start))
    n = gather(own_c, left, right, sems, wanted)
    parts = [slice(j * WIDE // PARTS, (j + 1) * WIDE // PARTS) for j in range(PARTS)]
    fetches = []
    for j, cols in enumerate(parts):
        if clear:
            acc[:, cols] = jnp.zeros((ROWS, WIDE // PARTS), jnp.float32)
        else:
            copy = pltpu.make_async_copy(before.at[:, cols], acc.at[:, cols], sems.at[2 + j])
            copy.start()
            fetches.append(copy)
    arrive(own_c, left, right, sems, n)
    stores = []
    for j, cols in enumerate(parts):
        if not clear:
            fetches[j].wait()
        contract(left, right, n, acc, cols)
        copy = pltpu.make_async_copy(acc.at[:, cols], out.at[:, cols], sems.at[2 + j])
        copy.start()
        stores.append(copy)
    for copy in stores:
        copy.wait()


def last_kernel(steps, table, own_c, before, turn, first, second, *refs):
    came = refs[:2 * len(steps)]
    out, left, right, acc, rows, mixed, total, sems = refs[2 * len(steps):]
    n = gather(own_c, left, right, sems, from_steps(table, steps, came))
    fetches = []
    for j in range(PARTS):
        cols = pl.ds(j * WIDE // PARTS, WIDE // PARTS)
        copy = pltpu.make_async_copy(before.at[:, cols], acc.at[:, cols], sems.at[2 + j])
        copy.start()
        fetches.append(copy)
    own = []
    for c, chunk in enumerate((first, second)):
        copy = pltpu.make_async_copy(chunk, rows.at[pl.ds(c * PER, PER)], sems.at[2 + PARTS + c])
        copy.start()
        own.append(copy)
    arrive(own_c, left, right, sems, n)
    for j, fetch in enumerate(fetches):
        fetch.wait()
        cols = slice(j * WIDE // PARTS, (j + 1) * WIDE // PARTS)
        contract(left, right, n, acc, cols)
        for k in range(WIDE // PARTS // 256):
            here = slice(cols.start + k * 256, cols.start + (k + 1) * 256)
            part = acc[:, here].astype(jnp.bfloat16)
            mixed[:, here] = jnp.dot(part, turn[...], preferred_element_type=jnp.float32).astype(jnp.bfloat16)

    for copy in own:
        copy.wait()
    total[...] = jnp.zeros_like(total)

    @pl.loop(0, ROWS // 32, unroll=4)
    def _(j):
        def stacked(load):
            halves = []
            for h in range(2):
                at = pl.multiple_of(j * 32 + h * 16, 16)
                halves.append(jnp.concatenate([load(at, slice(p * BS, (p + 1) * BS)) for p in range(AB)], axis=0))
            return jnp.concatenate(halves, axis=1)

        block = j // (BS // 32)
        total[...] += lax.dot_general(
            stacked(lambda at, cols: mixed[pl.ds(at, 16), cols]),
            stacked(lambda at, cols: rows[block, pl.ds(pl.multiple_of(at - block * BS, 16), 16), cols]),
            (((1,), (1,)), ((), ())),
            preferred_element_type=jnp.float32,
        )

    r = lax.broadcasted_iota(jnp.int32, (256, 256), 0)
    c = lax.broadcasted_iota(jnp.int32, (256, 256), 1)
    kept = jnp.where(r % 16 == c % 16, total[...], 0.0)
    kept = kept.reshape(16, 16, 256).sum(axis=1)
    rr = lax.broadcasted_iota(jnp.int32, (256, 16), 0)
    cc = lax.broadcasted_iota(jnp.int32, (256, 16), 1)
    pick_q = jnp.where(rr // 16 == cc, 1.0, 0.0)
    out[...] = jnp.dot(kept, pick_q, preferred_element_type=jnp.float32, precision=lax.Precision.HIGHEST)


def run(kernel, table, own_c, operands, vmem_operands, blocks, last):
    smem = pl.BlockSpec(memory_space=pltpu.SMEM)
    vmem = pl.BlockSpec(memory_space=pltpu.VMEM)
    hbm = pl.BlockSpec(memory_space=pl.ANY)
    scratch = [
        pltpu.VMEM((NB, BS, blocks * BS), jnp.bfloat16),
        pltpu.VMEM((blocks * BS, WIDE), jnp.bfloat16),
        pltpu.VMEM((ROWS, WIDE), jnp.float32),
    ]
    if last:
        scratch += [
            pltpu.VMEM((NB, BS, WIDE), jnp.bfloat16),
            pltpu.VMEM((ROWS, WIDE), jnp.bfloat16),
            pltpu.VMEM((256, 256), jnp.float32),
        ]
    scratch.append(pltpu.SemaphoreType.DMA((4 + PARTS,)))
    shape = (16, 16) if last else (ROWS, WIDE)
    return pl.pallas_call(
        kernel,
        out_shape=jax.ShapeDtypeStruct(shape, jnp.float32),
        in_specs=[smem, hbm] + [vmem if k in vmem_operands else hbm for k in range(len(operands))],
        out_specs=vmem if last else hbm,
        scratch_shapes=scratch,
        compiler_params=pltpu.CompilerParams(vmem_limit_bytes=VMEM_BYTES),
        cost_estimate=pl.CostEstimate(flops=0, bytes_accessed=1024, transcendentals=0),
    )(table, own_c, *operands)


def flatten_kernel(tile, out):
    out[0] = tile[0, 0, 0].reshape(BS, WIDE)


def flatten(integrals, chunk):
    return pl.pallas_call(
        flatten_kernel,
        grid=(PER,),
        out_shape=jax.ShapeDtypeStruct((PER, BS, WIDE), jnp.bfloat16),
        in_specs=[pl.BlockSpec((1, 1, 1, BS, AB, BS), lambda b: (0, 0, chunk * PER + b, 0, 0, 0))],
        out_specs=pl.BlockSpec((1, BS, WIDE), lambda b: (b, 0, 0)),
        cost_estimate=pl.CostEstimate(flops=0, bytes_accessed=8 * 1024 * 1024, transcendentals=0),
    )(integrals)


def per_device(integrals, block_list, pair_count, occupied, virtual):
    own_c = occupied[0]
    ao = lax.axis_index("ao")
    aux = lax.axis_index("aux")
    where = jnp.stack([ao, aux]).astype(jnp.int32)

    own = [flatten(integrals, 0)]
    lists = jnp.concatenate([block_list.reshape(1, 32), pair_count], axis=1)
    own[0], lists = lax.optimization_barrier((own[0], lists))
    lists = jnp.concatenate([lists, around(lists, 1)], axis=0)
    integrals, lists = lax.optimization_barrier((integrals, lists))
    own.append(flatten(integrals, 1))
    lists = jnp.concatenate([lists, around(lists, 2)], axis=0)
    lists = lax.ppermute(lists, "aux", [(g, g ^ 1) for g in range(8)])
    lists = jnp.concatenate([lists, around(lists, 1)], axis=0)
    lists = jnp.concatenate([lists, around(lists, 2)], axis=0)
    table = plan(lists, where)
    longest = table[0]

    last = [across(own[c], 1) for c in range(CHUNKS)]
    following = [across(own[c], -1) for c in range(CHUNKS)]
    first, _, table = lax.optimization_barrier((last[0], following[0], table))
    far = [across(first, 1), across(following[1], -1)]
    tiles = [own, following, far, last]

    came = []

    def add(acc, near, some):
        blocks = [chunk for tile in near for chunk in tiles[tile]] + [b for q in some for b in came[q]]
        return run(
            functools.partial(sum_kernel, near, some, acc is None), table, own_c,
            ([] if acc is None else [acc]) + blocks, (), 2 * SIDE + 2 * G * len(some), False,
        )

    acc = add(None, (0, 1, 3), ())
    table, acc, far[0] = lax.optimization_barrier((table, acc, far[0]))
    for q in range(ALWAYS):
        if q >= DELAY:
            acc = add(acc, (FAR,) if q == DELAY else (), (q - DELAY,))
            table, acc = lax.optimization_barrier((table, acc))
        up, down = pack(q, table, tiles, came)
        came.append(list(lax.optimization_barrier((around(up, 1), around(down, -1)))))
    acc = add(acc, (), (ALWAYS - 2,))

    block = virtual[0]
    zero = jnp.zeros_like(block)
    turn = jnp.concatenate(
        [jnp.concatenate([block, zero], axis=1), jnp.concatenate([zero, block], axis=1)], axis=0
    )

    def finish(some, came, acc, turn):
        return run(
            functools.partial(last_kernel, some), table, own_c,
            [acc, turn] + own + [b for q in some for b in came[q]], (1,), 2 * G * len(some), True,
        )

    def ending(extra):
        def branch(came, acc, turn):
            came = list(came)
            for q in range(ALWAYS, ALWAYS + extra):
                up, down = pack(q, table, tiles, came)
                came.append([around(up, 1), around(down, -1)])
            return finish(tuple(range(ALWAYS - 1, ALWAYS + extra)), came, acc, turn)
        return branch

    more = (longest > G * ALWAYS).astype(jnp.int32) + (longest > G * (ALWAYS + 1)).astype(jnp.int32)
    partial = lax.switch(more, [ending(extra) for extra in range(STEPS - ALWAYS + 1)], came, acc, turn)

    pieces = lax.all_to_all(partial.reshape(128, 2), AXES, split_axis=0, concat_axis=0, tiled=True)
    return pieces.sum(axis=0).reshape(1, 2)


def solution(mesh):
    placed = (
        P("ao", "aux", None, None, None, None),
        P("ao", None, None),
        P("ao", None),
        P("ao", None, None, None, None, None),
        P("aux", None, None),
    )
    return jax.shard_map(
        per_device, mesh=mesh, in_specs=placed, out_specs=P("ao", "aux"), check_vma=False
    )
```

profile of v0, /device:TPU:1, one launch (start us, length us, event | category | flops | bytes accessed | tf_op | source)
XLA Modules:
  0.0 186.7 jit_solution(8348516863151140384)
XLA Ops:
  0.0 2.6 %shard_map.55.refs_0_ = bf16[4,128,2048]{2,1,0:T(8,128)(2,1)S(1)} custom-call(bf16[1,1,8,128,16,128]{5,4,3,2,1,0:T(8,128)(2,1)} %tile.2), custom_call_target="tpu_custom_call" | custom-call | bytes 8388608 | tf_op jit(solution)/shard_map/pallas_call | solution.py:458
  2.8 2.0 %collective-permute-start.6 = (s32[1,48]{1,0:T(1,128)S(1)}, s32[1,48]{1,0:T(1,128)S(1)}, u32[]{:S(2)}, u32[]{:S(2)}) collective-permute-start(s32[1,48]{1,0:T(1,128)S(1)} %pad_add_fusion.4), channel_id=1, source_target_pairs={{0,32},{1,9},{2,34},{3,11},{4,36},{5,13},{6,38},{7,15},{8,40},{9,1... | collective-permute-start | bytes 584 | tf_op jit(solution)/shard_map/ppermute | solution.py:50
  4.9 1.6 collective-permute-start.11
  6.5 2.1 %collective-permute-start.12 = (bf16[4,128,2048]{2,1,0:T(8,128)(2,1)S(1)}, bf16[4,128,2048]{2,1,0:T(8,128)(2,1)}, u32[]{:S(2)}, u32[]{:S(2)}) collective-permute-start(bf16[4,128,2048]{2,1,0:T(8,128)(2,1)S(1)} %shard_map.55.refs_0_), channel_id=1, source_target_pairs={{0,24},{1,97},{2,26},{3,99},{4,28},{5,101},{6,30},{7,103},{8,0},{9... | collective-permute-start | bytes 6291464 | tf_op jit(solution)/shard_map/ppermute | solution.py:46
  8.7 4.0 %shard_map.57.refs_1_ = bf16[4,128,2048]{2,1,0:T(8,128)(2,1)} custom-call(bf16[1,1,8,128,16,128]{5,4,3,2,1,0:T(8,128)(2,1)} %tile.2), custom_call_target="tpu_custom_call" | custom-call | bytes 8388608 | tf_op jit(solution)/shard_map/pallas_call | solution.py:458
  12.7 2.4 %collective-permute-start.13 = (bf16[4,128,2048]{2,1,0:T(8,128)(2,1)}, bf16[4,128,2048]{2,1,0:T(8,128)(2,1)}, u32[]{:S(2)}, u32[]{:S(2)}) collective-permute-start(bf16[4,128,2048]{2,1,0:T(8,128)(2,1)} %shard_map.57.refs_1_), channel_id=1, source_target_pairs={{0,24},{1,97},{2,26},{3,99},{4,28},{5,101},{6,30},{7,103},{8,0},{9... | collective-permute-start | bytes 6291464 | tf_op jit(solution)/shard_map/ppermute | solution.py:46
  15.1 1.5 collective-permute-start.7
  16.6 2.5 %collective-permute-done.7 = s32[2,48]{1,0:T(2,128)S(1)} collective-permute-done((s32[2,48]{1,0:T(2,128)S(1)}, s32[2,48]{1,0:T(2,128)S(1)}, u32[]{:S(2)}, u32[]{:S(2)}) %collective-permute-start.7) | collective-permute-done | bytes 416 | tf_op jit(solution)/shard_map/ppermute | solution.py:50
  19.1 2.9 %collective-permute-start.8 = (s32[4,48]{1,0:T(4,128)S(1)}, s32[4,48]{1,0:T(4,128)S(1)}, u32[]{:S(2)}, u32[]{:S(2)}) collective-permute-start(s32[4,48]{1,0:T(4,128)S(1)} %pad_add_fusion.2), channel_id=1, source_target_pairs={{0,1},{1,0},{2,3},{3,2},{4,5},{5,4},{6,7},{7,6},{8,9},{9,8},{10,11... | collective-permute-start | bytes 2312 | tf_op jit(solution)/shard_map/ppermute | solution.py:481
  22.8 4.1 %collective-permute-done.9 = s32[4,48]{1,0:T(4,128)S(1)} collective-permute-done((s32[4,48]{1,0:T(4,128)S(1)}, s32[4,48]{1,0:T(4,128)S(1)}, u32[]{:S(2)}, u32[]{:S(2)}) %collective-permute-start.9) | collective-permute-done | bytes 800 | tf_op jit(solution)/shard_map/ppermute | solution.py:50
  27.7 3.4 %collective-permute-done.10 = s32[8,48]{1,0:T(8,128)S(1)} collective-permute-done((s32[8,48]{1,0:T(8,128)S(1)}, s32[8,48]{1,0:T(8,128)S(1)}, u32[]{:S(2)}, u32[]{:S(2)}) %collective-permute-start.10) | collective-permute-done | bytes 1568 | tf_op jit(solution)/shard_map/ppermute | solution.py:50
  31.7 7.4 %shard_map.56.table = s32[256]{0:T(256)S(1)} custom-call(s32[16,48]{1,0:T(8,128)} %pad_add_fusion.came, s32[2]{0:T(128)} %pad_add_fusion.5.where), custom_call_target="tpu_custom_call" | custom-call | tf_op jit(solution)/shard_map/pallas_call | solution.py:216
  39.1 15.4 %collective-permute-done.13.refs_3_ = bf16[4,128,2048]{2,1,0:T(8,128)(2,1)} collective-permute-done((bf16[4,128,2048]{2,1,0:T(8,128)(2,1)}, bf16[4,128,2048]{2,1,0:T(8,128)(2,1)}, u32[]{:S(2)}, u32[]{:S(2)}) %collective-permute-start.13) | collective-permute-done | bytes 2097184 | tf_op jit(solution)/shard_map/ppermute | solution.py:46
  54.5 3.2 %collective-permute-start.16 = (bf16[4,128,2048]{2,1,0:T(8,128)(2,1)}, bf16[4,128,2048]{2,1,0:T(8,128)(2,1)}, u32[]{:S(2)}, u32[]{:S(2)}) collective-permute-start(bf16[4,128,2048]{2,1,0:T(8,128)(2,1)} %collective-permute-done.13.refs_3_), channel_id=1, source_target_pairs={{0,24},{1,97},{2,26},{3,99},{4,28},{5,101},{6,30},{7,103},{8,0},{9... | collective-permute-start | bytes 6291464 | tf_op jit(solution)/shard_map/ppermute | solution.py:46
  57.7 9.6 %shard_map.58.refs_0_ = f32[1024,2048]{1,0:T(8,128)} custom-call(s32[256]{0:T(256)S(1)} %shard_map.56.table, bf16[8,16,2,128,128]{4,3,2,1,0:T(8,128)(2,1)} %bitcast.7, bf16[4,128,2048]{2,1,0:T(8,128)(2,1)S(1)} %shard_map.55.refs_0_, bf16[4,128,2048]{2,1,0:T(8,128)(2,1)} %shard_map.57.refs_1_, bf16[4,128,2048]{2,1,0:T(8,128)(2,1)} %collective-permute-done.12.refs_2_, ...), custom_call_target="tpu_custom_call" | custom-call | bytes 1024 | tf_op jit(solution)/shard_map/pallas_call | solution.py:442
  67.3 10.2 %collective-permute-done.15.refs_1_.refs_6_ = bf16[4,128,2048]{2,1,0:T(8,128)(2,1)} collective-permute-done((bf16[4,128,2048]{2,1,0:T(8,128)(2,1)}, bf16[4,128,2048]{2,1,0:T(8,128)(2,1)}, u32[]{:S(2)}, u32[]{:S(2)}) %collective-permute-start.15) | collective-permute-done | bytes 2097184 | tf_op jit(solution)/shard_map/ppermute | solution.py:46
  77.5 3.7 %shard_map.59 = (bf16[3,128,2048]{2,1,0:T(8,128)(2,1)}, bf16[3,128,2048]{2,1,0:T(8,128)(2,1)}) custom-call(s32[256]{0:T(256)S(1)} %shard_map.56.table, bf16[4,128,2048]{2,1,0:T(8,128)(2,1)S(1)} %shard_map.55.refs_0_, bf16[4,128,2048]{2,1,0:T(8,128)(2,1)} %shard_map.57.refs_1_, bf16[4,128,2048]{2,1,0:T(8,128)(2,1)} %collective-permute-done.12.refs_2_, ...), custom_call_target="tpu_custom_call" | custom-call | bytes 1024 | tf_op jit(solution)/shard_map/pallas_call | solution.py:261
  84.0 4.1 %shard_map.61 = (bf16[3,128,2048]{2,1,0:T(8,128)(2,1)}, bf16[3,128,2048]{2,1,0:T(8,128)(2,1)}) custom-call(s32[256]{0:T(256)S(1)} %shard_map.56.table, bf16[4,128,2048]{2,1,0:T(8,128)(2,1)S(1)} %shard_map.55.refs_0_, bf16[4,128,2048]{2,1,0:T(8,128)(2,1)} %shard_map.57.refs_1_, bf16[4,128,2048]{2,1,0:T(8,128)(2,1)} %collective-permute-done.12.refs_2_, ...), custom_call_target="tpu_custom_call" | custom-call | bytes 1024 | tf_op jit(solution)/shard_map/pallas_call | solution.py:261
  88.2 2.7 %collective-permute-start.20 = (bf16[3,128,2048]{2,1,0:T(8,128)(2,1)}, bf16[3,128,2048]{2,1,0:T(8,128)(2,1)}, u32[]{:S(2)}, u32[]{:S(2)}) collective-permute-start(bf16[3,128,2048]{2,1,0:T(8,128)(2,1)} %get-tuple-element.204), channel_id=1, source_target_pairs={{0,96},{1,25},{2,98},{3,27},{4,100},{5,29},{6,102},{7,31},{8,104},... | collective-permute-start | bytes 4718600 | tf_op jit(solution)/shard_map/ppermute | solution.py:50
  90.8 11.5 %collective-permute-done.17.refs_3_.refs_8_ = bf16[3,128,2048]{2,1,0:T(8,128)(2,1)} collective-permute-done((bf16[3,128,2048]{2,1,0:T(8,128)(2,1)}, bf16[3,128,2048]{2,1,0:T(8,128)(2,1)}, u32[]{:S(2)}, u32[]{:S(2)}) %collective-permute-start.17) | collective-permute-done | bytes 1572896 | tf_op jit(solution)/shard_map/ppermute | solution.py:50
  102.4 8.5 %shard_map.60.refs_0_ = f32[1024,2048]{1,0:T(8,128)} custom-call(s32[256]{0:T(256)S(1)} %shard_map.56.table, bf16[8,16,2,128,128]{4,3,2,1,0:T(8,128)(2,1)} %bitcast.8, f32[1024,2048]{1,0:T(8,128)} %shard_map.58.refs_0_, bf16[4,128,2048]{2,1,0:T(8,128)(2,1)} %collective-permute-done.15.refs_1_.refs_6_, ...), custom_call_target="tpu_custom_call" | custom-call | bytes 1024 | tf_op jit(solution)/shard_map/pallas_call | solution.py:442
  111.0 3.8 %shard_map.63 = (bf16[3,128,2048]{2,1,0:T(8,128)(2,1)}, bf16[3,128,2048]{2,1,0:T(8,128)(2,1)}) custom-call(s32[256]{0:T(256)S(1)} %shard_map.56.table, bf16[4,128,2048]{2,1,0:T(8,128)(2,1)S(1)} %shard_map.55.refs_0_, bf16[4,128,2048]{2,1,0:T(8,128)(2,1)} %shard_map.57.refs_1_, bf16[4,128,2048]{2,1,0:T(8,128)(2,1)} %collective-permute-done.12.refs_2_, ...), custom_call_target="tpu_custom_call" | custom-call | bytes 1024 | tf_op jit(solution)/shard_map/pallas_call | solution.py:261
  114.8 4.6 %collective-permute-start.21 = (bf16[3,128,2048]{2,1,0:T(8,128)(2,1)}, bf16[3,128,2048]{2,1,0:T(8,128)(2,1)}, u32[]{:S(2)}, u32[]{:S(2)}) collective-permute-start(bf16[3,128,2048]{2,1,0:T(8,128)(2,1)} %get-tuple-element.209), channel_id=1, source_target_pairs={{0,32},{1,9},{2,34},{3,11},{4,36},{5,13},{6,38},{7,15},{8,40},{9,1... | collective-permute-start | bytes 4718600 | tf_op jit(solution)/shard_map/ppermute | solution.py:50
  119.7 7.5 %shard_map.62.refs_0_ = f32[1024,2048]{1,0:T(8,128)} custom-call(s32[256]{0:T(256)S(1)} %shard_map.56.table, bf16[8,16,2,128,128]{4,3,2,1,0:T(8,128)(2,1)} %bitcast.9, f32[1024,2048]{1,0:T(8,128)} %shard_map.60.refs_0_, bf16[3,128,2048]{2,1,0:T(8,128)(2,1)} %collective-permute-done.19.refs_1_.refs_10_, ...), custom_call_target="tpu_custom_call" | custom-call | bytes 1024 | tf_op jit(solution)/shard_map/pallas_call | solution.py:442
  127.2 3.4 %shard_map.65 = (bf16[3,128,2048]{2,1,0:T(8,128)(2,1)}, bf16[3,128,2048]{2,1,0:T(8,128)(2,1)}) custom-call(s32[256]{0:T(256)S(1)} %shard_map.56.table, bf16[4,128,2048]{2,1,0:T(8,128)(2,1)S(1)} %shard_map.55.refs_0_, bf16[4,128,2048]{2,1,0:T(8,128)(2,1)} %shard_map.57.refs_1_, bf16[4,128,2048]{2,1,0:T(8,128)(2,1)} %collective-permute-done.12.refs_2_, ...), custom_call_target="tpu_custom_call" | custom-call | bytes 1024 | tf_op jit(solution)/shard_map/pallas_call | solution.py:261
  130.6 2.3 %collective-permute-start.23 = (bf16[3,128,2048]{2,1,0:T(8,128)(2,1)}, bf16[3,128,2048]{2,1,0:T(8,128)(2,1)}, u32[]{:S(2)}, u32[]{:S(2)}) collective-permute-start(bf16[3,128,2048]{2,1,0:T(8,128)(2,1)} %get-tuple-element.213), channel_id=1, source_target_pairs={{0,32},{1,9},{2,34},{3,11},{4,36},{5,13},{6,38},{7,15},{8,40},{9,1... | collective-permute-start | bytes 4718600 | tf_op jit(solution)/shard_map/ppermute | solution.py:50
  132.9 2.9 %collective-permute-start.24 = (bf16[3,128,2048]{2,1,0:T(8,128)(2,1)}, bf16[3,128,2048]{2,1,0:T(8,128)(2,1)}, u32[]{:S(2)}, u32[]{:S(2)}) collective-permute-start(bf16[3,128,2048]{2,1,0:T(8,128)(2,1)} %get-tuple-element.214), channel_id=1, source_target_pairs={{0,96},{1,25},{2,98},{3,27},{4,100},{5,29},{6,102},{7,31},{8,104},... | collective-permute-start | bytes 4718600 | tf_op jit(solution)/shard_map/ppermute | solution.py:50
  139.3 8.0 %shard_map.64 = f32[1024,2048]{1,0:T(8,128)} custom-call(s32[256]{0:T(256)S(1)} %shard_map.56.table, bf16[8,16,2,128,128]{4,3,2,1,0:T(8,128)(2,1)} %bitcast.10, f32[1024,2048]{1,0:T(8,128)} %shard_map.62.refs_0_, bf16[3,128,2048]{2,1,0:T(8,128)(2,1)} %collective-permute-done.21.refs_1_, bf16[3,128,2048]{2,1,0:T(8,128)(2,1)} %collective-permute-done.22.refs_2_), custom_call_target="tpu_custom_call" | custom-call | bytes 1024 | tf_op jit(solution)/shard_map/pallas_call | solution.py:442
  147.2 7.6 %collective-permute-done.23 = bf16[3,128,2048]{2,1,0:T(8,128)(2,1)} collective-permute-done((bf16[3,128,2048]{2,1,0:T(8,128)(2,1)}, bf16[3,128,2048]{2,1,0:T(8,128)(2,1)}, u32[]{:S(2)}, u32[]{:S(2)}) %collective-permute-start.23) | collective-permute-done | bytes 1572896 | tf_op jit(solution)/shard_map/ppermute | solution.py:50
  156.1 9.4 %conditional.1 = (f32[16,16]{1,0:T(8,128)S(1)}) conditional(s32[]{:T(128)} %bitcast.2, (s32[256]{0:T(256)S(1)}, bf16[8,16,2,128,128]{4,3,2,1,0:T(8,128)(2,1)}, f32[1024,2048]{1,0:T(8,128)}, bf16[256,256]{1,0:T(8,128)(2,1)S(1)}, bf16[4,128,2048]{2,1,0:T(8,128)(2,1)S(1)}, /*index=5*/bf16[4,128,2048]{2,1,0:T(8,128)(2,1)}, ...), branch_computations={%region_0.0_spmd, %region_1.0_spmd, %region_2.0_spmd} | conditional | bytes 37752032 | solution.py:534
  156.1 9.4 %branch_0_fun.1 = f32[16,16]{1,0:T(8,128)S(1)} custom-call(s32[256]{0:T(256)S(1)} %get-tuple-element.104.table, bf16[8,16,2,128,128]{4,3,2,1,0:T(8,128)(2,1)} %get-tuple-element.106.own_c, f32[1024,2048]{1,0:T(8,128)} %get-tuple-element.107.before, bf16[256,256]{1,0:T(8,128)(2,1)S(1)} %get-tuple-element.108.turn, ...), custom_call_target="tpu_custom_call" | custom-call | bytes 1024 | tf_op jit(solution)/shard_map/cond/branch_0_fun/pallas_call | solution.py:442
  165.6 20.4 %all_to_all.9 = f32[128,1,2]{2,1,0:T(1,128)S(1)} all-to-all(f32[128,1,2]{2,1,0:T(1,128)S(1)} %bitcast.14), channel_id=1, replica_groups=mesh['ao'=16,'aux'=8] {'ao','aux'}, dimensions={0} | all-to-all | bytes 2048 | tf_op jit(solution)/shard_map/all_to_all | solution.py:536
  (38 shorter events, 9.9 us)
Async XLA Ops:
  0.0 2.6 %copy-start.5 = (s32[1,16,2]{1,2,0:T(2,128)S(1)}, s32[1,16,2]{1,2,0:T(2,128)}, u32[]{:S(2)}) copy-start(s32[1,16,2]{1,2,0:T(2,128)} %param.9) | copy-start | bytes 388
  0.0 2.8 %copy-start.6 = (s32[1,16]{1,0:T(1,128)S(1)}, s32[1,16]{1,0:T(1,128)}, u32[]{:S(2)}) copy-start(s32[1,16]{1,0:T(1,128)} %param.10) | copy-start | bytes 196
  2.8 5.8 %collective-permute-start.6 = (s32[1,48]{1,0:T(1,128)S(1)}, s32[1,48]{1,0:T(1,128)S(1)}, u32[]{:S(2)}, u32[]{:S(2)}) collective-permute-start(s32[1,48]{1,0:T(1,128)S(1)} %pad_add_fusion.4), channel_id=1, source_target_pairs={{0,32},{1,9},{2,34},{3,11},{4,36},{5,13},{6,38},{7,15},{8,40},{9,1... | collective-permute-start | bytes 584 | tf_op jit(solution)/shard_map/ppermute | solution.py:50
  4.9 34.1 %collective-permute-start.11 = (bf16[4,128,2048]{2,1,0:T(8,128)(2,1)S(1)}, bf16[4,128,2048]{2,1,0:T(8,128)(2,1)}, u32[]{:S(2)}, u32[]{:S(2)}) collective-permute-start(bf16[4,128,2048]{2,1,0:T(8,128)(2,1)S(1)} %shard_map.55.refs_0_), channel_id=1, source_target_pairs={{0,8},{1,33},{2,10},{3,35},{4,12},{5,37},{6,14},{7,39},{8,16},{9,4... | collective-permute-start | bytes 6291464 | tf_op jit(solution)/shard_map/ppermute | solution.py:46
  6.5 32.5 %collective-permute-start.12 = (bf16[4,128,2048]{2,1,0:T(8,128)(2,1)S(1)}, bf16[4,128,2048]{2,1,0:T(8,128)(2,1)}, u32[]{:S(2)}, u32[]{:S(2)}) collective-permute-start(bf16[4,128,2048]{2,1,0:T(8,128)(2,1)S(1)} %shard_map.55.refs_0_), channel_id=1, source_target_pairs={{0,24},{1,97},{2,26},{3,99},{4,28},{5,101},{6,30},{7,103},{8,0},{9... | collective-permute-start | bytes 6291464 | tf_op jit(solution)/shard_map/ppermute | solution.py:46
  12.7 41.8 %collective-permute-start.13 = (bf16[4,128,2048]{2,1,0:T(8,128)(2,1)}, bf16[4,128,2048]{2,1,0:T(8,128)(2,1)}, u32[]{:S(2)}, u32[]{:S(2)}) collective-permute-start(bf16[4,128,2048]{2,1,0:T(8,128)(2,1)} %shard_map.57.refs_1_), channel_id=1, source_target_pairs={{0,24},{1,97},{2,26},{3,99},{4,28},{5,101},{6,30},{7,103},{8,0},{9... | collective-permute-start | bytes 6291464 | tf_op jit(solution)/shard_map/ppermute | solution.py:46
  15.1 4.0 %collective-permute-start.7 = (s32[2,48]{1,0:T(2,128)S(1)}, s32[2,48]{1,0:T(2,128)S(1)}, u32[]{:S(2)}, u32[]{:S(2)}) collective-permute-start(s32[2,48]{1,0:T(2,128)S(1)} %pad_add_fusion.3), channel_id=1, source_target_pairs={{0,64},{1,17},{2,66},{3,19},{4,68},{5,21},{6,70},{7,23},{8,72},{9,... | collective-permute-start | bytes 1160 | tf_op jit(solution)/shard_map/ppermute | solution.py:50
  19.1 3.7 %collective-permute-start.8 = (s32[4,48]{1,0:T(4,128)S(1)}, s32[4,48]{1,0:T(4,128)S(1)}, u32[]{:S(2)}, u32[]{:S(2)}) collective-permute-start(s32[4,48]{1,0:T(4,128)S(1)} %pad_add_fusion.2), channel_id=1, source_target_pairs={{0,1},{1,0},{2,3},{3,2},{4,5},{5,4},{6,7},{7,6},{8,9},{9,8},{10,11... | collective-permute-start | bytes 2312 | tf_op jit(solution)/shard_map/ppermute | solution.py:481
  22.8 4.1 %collective-permute-start.9 = (s32[4,48]{1,0:T(4,128)S(1)}, s32[4,48]{1,0:T(4,128)S(1)}, u32[]{:S(2)}, u32[]{:S(2)}) collective-permute-start(s32[4,48]{1,0:T(4,128)S(1)} %collective-permute-done.8), channel_id=1, source_target_pairs={{0,32},{1,9},{2,34},{3,11},{4,36},{5,13},{6,38},{7,15},{8,40},{9,1... | collective-permute-start | bytes 2312 | tf_op jit(solution)/shard_map/ppermute | solution.py:50
  26.9 4.1 %collective-permute-start.10 = (s32[8,48]{1,0:T(8,128)S(1)}, s32[8,48]{1,0:T(8,128)S(1)}, u32[]{:S(2)}, u32[]{:S(2)}) collective-permute-start(s32[8,48]{1,0:T(8,128)S(1)} %pad_add_fusion.1), channel_id=1, source_target_pairs={{0,64},{1,17},{2,66},{3,19},{4,68},{5,21},{6,70},{7,23},{8,72},{9,... | collective-permute-start | bytes 4616 | tf_op jit(solution)/shard_map/ppermute | solution.py:50
  27.6 30.1 %collective-permute-start.14 = (bf16[4,128,2048]{2,1,0:T(8,128)(2,1)}, bf16[4,128,2048]{2,1,0:T(8,128)(2,1)}, u32[]{:S(2)}, u32[]{:S(2)}) collective-permute-start(bf16[4,128,2048]{2,1,0:T(8,128)(2,1)} %shard_map.57.refs_1_), channel_id=1, source_target_pairs={{0,8},{1,33},{2,10},{3,35},{4,12},{5,37},{6,14},{7,39},{8,16},{9,4... | collective-permute-start | bytes 6291464 | tf_op jit(solution)/shard_map/ppermute | solution.py:46
  39.0 38.4 %collective-permute-start.15 = (bf16[4,128,2048]{2,1,0:T(8,128)(2,1)}, bf16[4,128,2048]{2,1,0:T(8,128)(2,1)}, u32[]{:S(2)}, u32[]{:S(2)}) collective-permute-start(bf16[4,128,2048]{2,1,0:T(8,128)(2,1)} %collective-permute-done.11.refs_4_), channel_id=1, source_target_pairs={{0,8},{1,33},{2,10},{3,35},{4,12},{5,37},{6,14},{7,39},{8,16},{9,4... | collective-permute-start | bytes 6291464 | tf_op jit(solution)/shard_map/ppermute | solution.py:46
  54.5 29.5 %collective-permute-start.16 = (bf16[4,128,2048]{2,1,0:T(8,128)(2,1)}, bf16[4,128,2048]{2,1,0:T(8,128)(2,1)}, u32[]{:S(2)}, u32[]{:S(2)}) collective-permute-start(bf16[4,128,2048]{2,1,0:T(8,128)(2,1)} %collective-permute-done.13.refs_3_), channel_id=1, source_target_pairs={{0,24},{1,97},{2,26},{3,99},{4,28},{5,101},{6,30},{7,103},{8,0},{9... | collective-permute-start | bytes 6291464 | tf_op jit(solution)/shard_map/ppermute | solution.py:46
  81.2 21.2 %collective-permute-start.17 = (bf16[3,128,2048]{2,1,0:T(8,128)(2,1)}, bf16[3,128,2048]{2,1,0:T(8,128)(2,1)}, u32[]{:S(2)}, u32[]{:S(2)}) collective-permute-start(bf16[3,128,2048]{2,1,0:T(8,128)(2,1)} %get-tuple-element.197), channel_id=1, source_target_pairs={{0,32},{1,9},{2,34},{3,11},{4,36},{5,13},{6,38},{7,15},{8,40},{9,1... | collective-permute-start | bytes 4718600 | tf_op jit(solution)/shard_map/ppermute | solution.py:50
  82.5 19.9 %collective-permute-start.18 = (bf16[3,128,2048]{2,1,0:T(8,128)(2,1)}, bf16[3,128,2048]{2,1,0:T(8,128)(2,1)}, u32[]{:S(2)}, u32[]{:S(2)}) collective-permute-start(bf16[3,128,2048]{2,1,0:T(8,128)(2,1)} %get-tuple-element.198), channel_id=1, source_target_pairs={{0,96},{1,25},{2,98},{3,27},{4,100},{5,29},{6,102},{7,31},{8,104},... | collective-permute-start | bytes 4718600 | tf_op jit(solution)/shard_map/ppermute | solution.py:50
  88.1 31.6 %collective-permute-start.19 = (bf16[3,128,2048]{2,1,0:T(8,128)(2,1)}, bf16[3,128,2048]{2,1,0:T(8,128)(2,1)}, u32[]{:S(2)}, u32[]{:S(2)}) collective-permute-start(bf16[3,128,2048]{2,1,0:T(8,128)(2,1)} %get-tuple-element.203), channel_id=1, source_target_pairs={{0,32},{1,9},{2,34},{3,11},{4,36},{5,13},{6,38},{7,15},{8,40},{9,1... | collective-permute-start | bytes 4718600 | tf_op jit(solution)/shard_map/ppermute | solution.py:50
  88.2 31.5 %collective-permute-start.20 = (bf16[3,128,2048]{2,1,0:T(8,128)(2,1)}, bf16[3,128,2048]{2,1,0:T(8,128)(2,1)}, u32[]{:S(2)}, u32[]{:S(2)}) collective-permute-start(bf16[3,128,2048]{2,1,0:T(8,128)(2,1)} %get-tuple-element.204), channel_id=1, source_target_pairs={{0,96},{1,25},{2,98},{3,27},{4,100},{5,29},{6,102},{7,31},{8,104},... | collective-permute-start | bytes 4718600 | tf_op jit(solution)/shard_map/ppermute | solution.py:50
  114.8 23.3 %collective-permute-start.21 = (bf16[3,128,2048]{2,1,0:T(8,128)(2,1)}, bf16[3,128,2048]{2,1,0:T(8,128)(2,1)}, u32[]{:S(2)}, u32[]{:S(2)}) collective-permute-start(bf16[3,128,2048]{2,1,0:T(8,128)(2,1)} %get-tuple-element.209), channel_id=1, source_target_pairs={{0,32},{1,9},{2,34},{3,11},{4,36},{5,13},{6,38},{7,15},{8,40},{9,1... | collective-permute-start | bytes 4718600 | tf_op jit(solution)/shard_map/ppermute | solution.py:50
  119.4 19.9 %collective-permute-start.22 = (bf16[3,128,2048]{2,1,0:T(8,128)(2,1)}, bf16[3,128,2048]{2,1,0:T(8,128)(2,1)}, u32[]{:S(2)}, u32[]{:S(2)}) collective-permute-start(bf16[3,128,2048]{2,1,0:T(8,128)(2,1)} %get-tuple-element.210), channel_id=1, source_target_pairs={{0,96},{1,25},{2,98},{3,27},{4,100},{5,29},{6,102},{7,31},{8,104},... | collective-permute-start | bytes 4718600 | tf_op jit(solution)/shard_map/ppermute | solution.py:50
  127.2 8.6 %copy-start.4 = (bf16[1,128,128]{2,1,0:T(8,128)(2,1)S(1)}, bf16[1,128,128]{2,1,0:T(8,128)(2,1)}, u32[]{:S(2)}) copy-start(bf16[1,128,128]{2,1,0:T(8,128)(2,1)} %param.12) | copy-start | bytes 98308
  130.6 24.3 %collective-permute-start.23 = (bf16[3,128,2048]{2,1,0:T(8,128)(2,1)}, bf16[3,128,2048]{2,1,0:T(8,128)(2,1)}, u32[]{:S(2)}, u32[]{:S(2)}) collective-permute-start(bf16[3,128,2048]{2,1,0:T(8,128)(2,1)} %get-tuple-element.213), channel_id=1, source_target_pairs={{0,32},{1,9},{2,34},{3,11},{4,36},{5,13},{6,38},{7,15},{8,40},{9,1... | collective-permute-start | bytes 4718600 | tf_op jit(solution)/shard_map/ppermute | solution.py:50
  132.9 23.2 %collective-permute-start.24 = (bf16[3,128,2048]{2,1,0:T(8,128)(2,1)}, bf16[3,128,2048]{2,1,0:T(8,128)(2,1)}, u32[]{:S(2)}, u32[]{:S(2)}) collective-permute-start(bf16[3,128,2048]{2,1,0:T(8,128)(2,1)} %get-tuple-element.214), channel_id=1, source_target_pairs={{0,96},{1,25},{2,98},{3,27},{4,100},{5,29},{6,102},{7,31},{8,104},... | collective-permute-start | bytes 4718600 | tf_op jit(solution)/shard_map/ppermute | solution.py:50
where the time goes:
time: 188 us; the launch traced here: 187 us
  Pallas kernels  71.9 us (38%)
  waiting for transfers between devices  58.6 us (31%)
  starting transfers between devices  31.6 us (17%)
  blocking collectives  20.4 us (11%)
  other arithmetic  1.99 us (1%)
    pallas_call x5, Pallas kernels, run(): pl.pallas_call(kernel, out_shape=jax.ShapeDtypeStruct(shape, jnp.float32)...  42.9 us
    ppermute x12, waiting for transfers between devices, around(): return lax.ppermute(array, AXES, shift(True, step))  32.1 us
    ppermute x6, waiting for transfers between devices, across(): return lax.ppermute(array, AXES, shift(False, step))  25.6 us
    all_to_all x1, blocking collectives, per_device(): lax.all_to_all(partial.reshape(128, 2), AXES, split_axis=0, concat_axis=0...  20.4 us
    ppermute x12, starting transfers between devices, around(): return lax.ppermute(array, AXES, shift(True, step))  19.3 us
    pallas_call x4, Pallas kernels, pack(): pl.pallas_call(functools.partial(pack_kernel, step, held, relays), out_sh...  15 us
    ppermute x6, starting transfers between devices, across(): return lax.ppermute(array, AXES, shift(False, step))  9.41 us
    pallas_call x1, Pallas kernels, plan(): pl.pallas_call(plan_kernel, out_shape=jax.ShapeDtypeStruct((256,), jnp.in...  7.35 us
  transfers between devices with their start and end apart: 19, of which 11 were waited for; matrix products, arithmetic and copies ran while one was open for 1% of the time, Pallas kernels for 32%

commit v1 on v0

--- a/solution.py
+++ b/solution.py
@@ -226,33 +226,42 @@
     refs = list(refs)
     tiles = {m: [refs.pop(0) for _ in range(CHUNKS)] for m in held}
     came = [refs.pop(0) for _ in range(2 * relays)]
-    up, down, sems = refs
-    waits = []
+    up, down, room, sems = refs
+    arrivals, leavings = [], []
     for way, out in enumerate((up, down)):
         for h in range(G):
+            k = G * way + h
             code = table[SEND + 24 * way + G * step + h]
-            dst = out.at[h]
-            sem = sems.at[G * way + h]
-            for m in held:
-                for c, tile in enumerate(tiles[m]):
-                    @pl.when(code // PER == m * CHUNKS + c)
-                    def _(tile=tile, dst=dst, sem=sem, code=code):
-                        pltpu.make_async_copy(tile.at[code % PER], dst, sem).start()
-            for q in range(relays):
-                for g in range(G):
-                    @pl.when(code == RELAY + G * q + g)
-                    def _(q=q, g=g, way=way, dst=dst, sem=sem):
-                        pltpu.make_async_copy(came[2 * q + way].at[g], dst, sem).start()
-            waits.append(pltpu.make_async_copy(tiles[0][0].at[0], dst, sem))
-    for copy in waits:
-        copy.wait()
+            dst = room.at[k]
+
+            @pl.when(code < RELAY)
+            def _(code=code, dst=dst, k=k):
+                for m in held:
+                    for c, tile in enumerate(tiles[m]):
+                        @pl.when(code // PER == m * CHUNKS + c)
+                        def _():
+                            pltpu.make_async_copy(tile.at[code % PER], dst, sems.at[k]).start()
+
+            @pl.when(code >= RELAY)
+            def _(code=code, dst=dst, k=k, way=way):
+                for q in range(relays):
+                    @pl.when((code - RELAY) // G == q)
+                    def _():
+                        pltpu.make_async_copy(came[2 * q + way].at[(code - RELAY) % G], dst, sems.at[k]).start()
+
+            arrivals.append(pltpu.make_async_copy(tiles[0][0].at[0], dst, sems.at[k]))
+            leavings.append(pltpu.make_async_copy(dst, out.at[h], sems.at[2 * G + k]))
+    for arrival, leaving in zip(arrivals, leavings):
+        arrival.wait()
+        leaving.start()
+    for leaving in leavings:
+        leaving.wait()
 
 
 def pack(step, table, tiles, came):
     relays = max(step - DELAY + 1, 0)
     held = [m for m in ORDER if G * step >= FIRST or m != FAR]
     smem = pl.BlockSpec(memory_space=pltpu.SMEM)
-    vmem = pl.BlockSpec(memory_space=pltpu.VMEM)
     hbm = pl.BlockSpec(memory_space=pl.ANY)
     operands = [chunk for m in held for chunk in tiles[m]]
     for q in range(relays):
@@ -262,8 +271,8 @@
         functools.partial(pack_kernel, step, held, relays),
         out_shape=[shape, shape],
         in_specs=[smem] + [hbm] * len(operands),
-        out_specs=[vmem, vmem],
-        scratch_shapes=[pltpu.SemaphoreType.DMA((2 * G,))],
+        out_specs=[hbm, hbm],
+        scratch_shapes=[pltpu.VMEM((2 * G, BS, WIDE), jnp.bfloat16), pltpu.SemaphoreType.DMA((4 * G,))],
         cost_estimate=pl.CostEstimate(flops=0, bytes_accessed=1024, transcendentals=0),
     )(table, *operands)
 
@@ -368,7 +377,7 @@
 
 def last_kernel(steps, table, own_c, before, turn, first, second, *refs):
     came = refs[:2 * len(steps)]
-    out, left, right, acc, rows, mixed, total, sems = refs[2 * len(steps):]
+    out, left, right, acc, rows, part, mixed, total, sems = refs[2 * len(steps):]
     n = gather(own_c, left, right, sems, from_steps(table, steps, came))
     fetches = []
     for j in range(PARTS):
@@ -382,14 +391,29 @@
         copy.start()
         own.append(copy)
     arrive(own_c, left, right, sems, n)
+    pairs = (n + 1) // 2
     for j, fetch in enumerate(fetches):
         fetch.wait()
         cols = slice(j * WIDE // PARTS, (j + 1) * WIDE // PARTS)
-        contract(left, right, n, acc, cols)
+
+        @pl.when(pairs == 0)
+        def _():
+            part[:, cols] = acc[:, cols].astype(jnp.bfloat16)
+
+        for p in range(1, G * len(steps) + 1):
+            @pl.when(pairs == p)
+            def _():
+                added = jnp.dot(
+                    left[:, :, :2 * p * BS].reshape(ROWS, 2 * p * BS), right[:2 * p * BS, cols],
+                    preferred_element_type=jnp.float32,
+                )
+                part[:, cols] = (acc[:, cols] + added).astype(jnp.bfloat16)
+
         for k in range(WIDE // PARTS // 256):
             here = slice(cols.start + k * 256, cols.start + (k + 1) * 256)
-            part = acc[:, here].astype(jnp.bfloat16)
-            mixed[:, here] = jnp.dot(part, turn[...], preferred_element_type=jnp.float32).astype(jnp.bfloat16)
+            mixed[:, here] = jnp.dot(
+                part[:, here], turn[...], preferred_element_type=jnp.float32
+            ).astype(jnp.bfloat16)
 
     for copy in own:
         copy.wait()
@@ -434,6 +458,7 @@
     if last:
         scratch += [
             pltpu.VMEM((NB, BS, WIDE), jnp.bfloat16),
+            pltpu.VMEM((ROWS, WIDE), jnp.bfloat16),
             pltpu.VMEM((ROWS, WIDE), jnp.bfloat16),
             pltpu.VMEM((256, 256), jnp.float32),
         ]
@@ -502,10 +527,10 @@
     acc = add(None, (0, 1, 3), ())
     table, acc, far[0] = lax.optimization_barrier((table, acc, far[0]))
     for q in range(ALWAYS):
-        if q >= DELAY:
-            acc = add(acc, (FAR,) if q == DELAY else (), (q - DELAY,))
-            table, acc = lax.optimization_barrier((table, acc))
         up, down = pack(q, table, tiles, came)
+        if q == ALWAYS - 1:
+            up, down, acc = lax.optimization_barrier((up, down, acc))
+            acc = add(acc, (FAR,), tuple(range(q - 1)))
         came.append(list(lax.optimization_barrier((around(up, 1), around(down, -1)))))
     acc = add(acc, (), (ALWAYS - 2,))
 

time: 188 us -> 183 us (0.973); the launches traced: 187 us -> 184 us
  waiting for transfers between devices: 58.6 us -> 67.3 us
  Pallas kernels: 71.9 us -> 64.8 us
  starting transfers between devices: 31.6 us -> 27.1 us
    pallas_call x5 -> x4, Pallas kernels: 42.9 us -> 36.1 us  [run(): pl.pallas_call(kernel, out_shape=jax.ShapeDtypeStruct(shape, jnp.float32)...]
    ppermute x12, waiting for transfers between devices: 32.1 us -> 37 us  [around(): return lax.ppermute(array, AXES, shift(True, step))]
    ppermute x12, starting transfers between devices: 19.3 us -> 14.8 us  [around(): return lax.ppermute(array, AXES, shift(True, step))]
    ppermute x6, waiting for transfers between devices: 25.6 us -> 29.4 us  [across(): return lax.ppermute(array, AXES, shift(False, step))]
  transfers between devices with their start and end apart: 19 -> 19, of which waited for: 11 -> 9; matrix products, arithmetic and copies ran while one was open for 1% -> 1% of each run, Pallas kernels for 32% -> 29%
where the time goes in v1:
time: 183 us; the launch traced here: 184 us
  waiting for transfers between devices  67.3 us (37%)
  Pallas kernels  64.8 us (35%)
  starting transfers between devices  27.1 us (15%)
  blocking collectives  20 us (11%)
  other arithmetic  1.99 us (1%)
    ppermute x12, waiting for transfers between devices, around(): return lax.ppermute(array, AXES, shift(True, step))  37 us
    pallas_call x4, Pallas kernels, run(): pl.pallas_call(kernel, out_shape=jax.ShapeDtypeStruct(shape, jnp.float32)...  36.1 us
    ppermute x6, waiting for transfers between devices, across(): return lax.ppermute(array, AXES, shift(False, step))  29.4 us
    all_to_all x1, blocking collectives, per_device(): lax.all_to_all(partial.reshape(128, 2), AXES, split_axis=0, concat_axis=0...  20 us
    pallas_call x4, Pallas kernels, pack(): pl.pallas_call(functools.partial(pack_kernel, step, held, relays), out_sh...  14.8 us
    ppermute x12, starting transfers between devices, around(): return lax.ppermute(array, AXES, shift(True, step))  14.8 us
    ppermute x6, starting transfers between devices, across(): return lax.ppermute(array, AXES, shift(False, step))  9.44 us
    pallas_call x1, Pallas kernels, plan(): pl.pallas_call(plan_kernel, out_shape=jax.ShapeDtypeStruct((256,), jnp.in...  7.34 us
  transfers between devices with their start and end apart: 19, of which 9 were waited for; matrix products, arithmetic and copies ran while one was open for 1% of the time, Pallas kernels for 29%

profile of v1, /device:TPU:1, one launch (start us, length us, event | category | flops | bytes accessed | tf_op | source)
XLA Modules:
  0.0 183.6 jit_solution(15477584840447482262)
XLA Ops:
  0.0 2.6 %shard_map.55.refs_0_ = bf16[4,128,2048]{2,1,0:T(8,128)(2,1)S(1)} custom-call(bf16[1,1,8,128,16,128]{5,4,3,2,1,0:T(8,128)(2,1)} %tile.2), custom_call_target="tpu_custom_call" | custom-call | bytes 8388608 | tf_op jit(solution)/shard_map/pallas_call | solution.py:483
  2.8 2.0 %collective-permute-start.6 = (s32[1,48]{1,0:T(1,128)S(1)}, s32[1,48]{1,0:T(1,128)S(1)}, u32[]{:S(2)}, u32[]{:S(2)}) collective-permute-start(s32[1,48]{1,0:T(1,128)S(1)} %pad_add_fusion.4), channel_id=1, source_target_pairs={{0,32},{1,9},{2,34},{3,11},{4,36},{5,13},{6,38},{7,15},{8,40},{9,1... | collective-permute-start | bytes 584 | tf_op jit(solution)/shard_map/ppermute | solution.py:50
  4.9 1.6 collective-permute-start.11
  6.5 2.1 %collective-permute-start.12 = (bf16[4,128,2048]{2,1,0:T(8,128)(2,1)S(1)}, bf16[4,128,2048]{2,1,0:T(8,128)(2,1)}, u32[]{:S(2)}, u32[]{:S(2)}) collective-permute-start(bf16[4,128,2048]{2,1,0:T(8,128)(2,1)S(1)} %shard_map.55.refs_0_), channel_id=1, source_target_pairs={{0,24},{1,97},{2,26},{3,99},{4,28},{5,101},{6,30},{7,103},{8,0},{9... | collective-permute-start | bytes 6291464 | tf_op jit(solution)/shard_map/ppermute | solution.py:46
  8.7 4.0 %shard_map.57.refs_1_ = bf16[4,128,2048]{2,1,0:T(8,128)(2,1)} custom-call(bf16[1,1,8,128,16,128]{5,4,3,2,1,0:T(8,128)(2,1)} %tile.2), custom_call_target="tpu_custom_call" | custom-call | bytes 8388608 | tf_op jit(solution)/shard_map/pallas_call | solution.py:483
  12.6 2.4 %collective-permute-start.13 = (bf16[4,128,2048]{2,1,0:T(8,128)(2,1)}, bf16[4,128,2048]{2,1,0:T(8,128)(2,1)}, u32[]{:S(2)}, u32[]{:S(2)}) collective-permute-start(bf16[4,128,2048]{2,1,0:T(8,128)(2,1)} %shard_map.57.refs_1_), channel_id=1, source_target_pairs={{0,24},{1,97},{2,26},{3,99},{4,28},{5,101},{6,30},{7,103},{8,0},{9... | collective-permute-start | bytes 6291464 | tf_op jit(solution)/shard_map/ppermute | solution.py:46
  15.0 1.5 collective-permute-start.7
  16.5 2.5 %collective-permute-done.7 = s32[2,48]{1,0:T(2,128)S(1)} collective-permute-done((s32[2,48]{1,0:T(2,128)S(1)}, s32[2,48]{1,0:T(2,128)S(1)}, u32[]{:S(2)}, u32[]{:S(2)}) %collective-permute-start.7) | collective-permute-done | bytes 416 | tf_op jit(solution)/shard_map/ppermute | solution.py:50
  19.0 2.9 %collective-permute-start.8 = (s32[4,48]{1,0:T(4,128)S(1)}, s32[4,48]{1,0:T(4,128)S(1)}, u32[]{:S(2)}, u32[]{:S(2)}) collective-permute-start(s32[4,48]{1,0:T(4,128)S(1)} %pad_add_fusion.2), channel_id=1, source_target_pairs={{0,1},{1,0},{2,3},{3,2},{4,5},{5,4},{6,7},{7,6},{8,9},{9,8},{10,11... | collective-permute-start | bytes 2312 | tf_op jit(solution)/shard_map/ppermute | solution.py:506
  22.7 4.1 %collective-permute-done.9 = s32[4,48]{1,0:T(4,128)S(1)} collective-permute-done((s32[4,48]{1,0:T(4,128)S(1)}, s32[4,48]{1,0:T(4,128)S(1)}, u32[]{:S(2)}, u32[]{:S(2)}) %collective-permute-start.9) | collective-permute-done | bytes 800 | tf_op jit(solution)/shard_map/ppermute | solution.py:50
  27.6 3.4 %collective-permute-done.10 = s32[8,48]{1,0:T(8,128)S(1)} collective-permute-done((s32[8,48]{1,0:T(8,128)S(1)}, s32[8,48]{1,0:T(8,128)S(1)}, u32[]{:S(2)}, u32[]{:S(2)}) %collective-permute-start.10) | collective-permute-done | bytes 1568 | tf_op jit(solution)/shard_map/ppermute | solution.py:50
  31.6 7.3 %shard_map.56.table = s32[256]{0:T(256)S(1)} custom-call(s32[16,48]{1,0:T(8,128)} %pad_add_fusion.came, s32[2]{0:T(128)} %pad_add_fusion.5.where), custom_call_target="tpu_custom_call" | custom-call | tf_op jit(solution)/shard_map/pallas_call | solution.py:216
  39.1 15.4 %collective-permute-done.13.refs_3_ = bf16[4,128,2048]{2,1,0:T(8,128)(2,1)} collective-permute-done((bf16[4,128,2048]{2,1,0:T(8,128)(2,1)}, bf16[4,128,2048]{2,1,0:T(8,128)(2,1)}, u32[]{:S(2)}, u32[]{:S(2)}) %collective-permute-start.13) | collective-permute-done | bytes 2097184 | tf_op jit(solution)/shard_map/ppermute | solution.py:46
  54.5 3.2 %collective-permute-start.16 = (bf16[4,128,2048]{2,1,0:T(8,128)(2,1)}, bf16[4,128,2048]{2,1,0:T(8,128)(2,1)}, u32[]{:S(2)}, u32[]{:S(2)}) collective-permute-start(bf16[4,128,2048]{2,1,0:T(8,128)(2,1)} %collective-permute-done.13.refs_3_), channel_id=1, source_target_pairs={{0,24},{1,97},{2,26},{3,99},{4,28},{5,101},{6,30},{7,103},{8,0},{9... | collective-permute-start | bytes 6291464 | tf_op jit(solution)/shard_map/ppermute | solution.py:46
  57.7 5.8 %shard_map.58.refs_0_ = f32[1024,2048]{1,0:T(8,128)} custom-call(s32[256]{0:T(256)S(1)} %shard_map.56.table, bf16[8,16,2,128,128]{4,3,2,1,0:T(8,128)(2,1)} %bitcast.7, bf16[4,128,2048]{2,1,0:T(8,128)(2,1)S(1)} %shard_map.55.refs_0_, bf16[4,128,2048]{2,1,0:T(8,128)(2,1)} %shard_map.57.refs_1_, bf16[4,128,2048]{2,1,0:T(8,128)(2,1)} %collective-permute-done.12.refs_2_, ...), custom_call_target="tpu_custom_call" | custom-call | bytes 1024 | tf_op jit(solution)/shard_map/pallas_call | solution.py:467
  63.5 14.0 %collective-permute-done.15.refs_6_.refs_1_ = bf16[4,128,2048]{2,1,0:T(8,128)(2,1)} collective-permute-done((bf16[4,128,2048]{2,1,0:T(8,128)(2,1)}, bf16[4,128,2048]{2,1,0:T(8,128)(2,1)}, u32[]{:S(2)}, u32[]{:S(2)}) %collective-permute-start.15) | collective-permute-done | bytes 2097184 | tf_op jit(solution)/shard_map/ppermute | solution.py:46
  77.5 4.1 %shard_map.59 = (bf16[3,128,2048]{2,1,0:T(8,128)(2,1)}, bf16[3,128,2048]{2,1,0:T(8,128)(2,1)}) custom-call(s32[256]{0:T(256)S(1)} %shard_map.56.table, bf16[4,128,2048]{2,1,0:T(8,128)(2,1)S(1)} %shard_map.55.refs_0_, bf16[4,128,2048]{2,1,0:T(8,128)(2,1)} %shard_map.57.refs_1_, bf16[4,128,2048]{2,1,0:T(8,128)(2,1)} %collective-permute-done.12.refs_2_, ...), custom_call_target="tpu_custom_call" | custom-call | bytes 1024 | tf_op jit(solution)/shard_map/pallas_call | solution.py:270
  81.8 2.5 %collective-permute-start.18 = (bf16[3,128,2048]{2,1,0:T(8,128)(2,1)}, bf16[3,128,2048]{2,1,0:T(8,128)(2,1)}, u32[]{:S(2)}, u32[]{:S(2)}) collective-permute-start(bf16[3,128,2048]{2,1,0:T(8,128)(2,1)} %get-tuple-element.196), channel_id=1, source_target_pairs={{0,96},{1,25},{2,98},{3,27},{4,100},{5,29},{6,102},{7,31},{8,104},... | collective-permute-start | bytes 4718600 | tf_op jit(solution)/shard_map/ppermute | solution.py:50
  84.3 3.4 %shard_map.60 = (bf16[3,128,2048]{2,1,0:T(8,128)(2,1)}, bf16[3,128,2048]{2,1,0:T(8,128)(2,1)}) custom-call(s32[256]{0:T(256)S(1)} %shard_map.56.table, bf16[4,128,2048]{2,1,0:T(8,128)(2,1)S(1)} %shard_map.55.refs_0_, bf16[4,128,2048]{2,1,0:T(8,128)(2,1)} %shard_map.57.refs_1_, bf16[4,128,2048]{2,1,0:T(8,128)(2,1)} %collective-permute-done.12.refs_2_, ...), custom_call_target="tpu_custom_call" | custom-call | bytes 1024 | tf_op jit(solution)/shard_map/pallas_call | solution.py:270
  87.8 2.7 %collective-permute-start.20 = (bf16[3,128,2048]{2,1,0:T(8,128)(2,1)}, bf16[3,128,2048]{2,1,0:T(8,128)(2,1)}, u32[]{:S(2)}, u32[]{:S(2)}) collective-permute-start(bf16[3,128,2048]{2,1,0:T(8,128)(2,1)} %get-tuple-element.200), channel_id=1, source_target_pairs={{0,96},{1,25},{2,98},{3,27},{4,100},{5,29},{6,102},{7,31},{8,104},... | collective-permute-start | bytes 4718600 | tf_op jit(solution)/shard_map/ppermute | solution.py:50
  90.5 12.2 %collective-permute-done.17.refs_8_.refs_3_ = bf16[3,128,2048]{2,1,0:T(8,128)(2,1)} collective-permute-done((bf16[3,128,2048]{2,1,0:T(8,128)(2,1)}, bf16[3,128,2048]{2,1,0:T(8,128)(2,1)}, u32[]{:S(2)}, u32[]{:S(2)}) %collective-permute-start.17) | collective-permute-done | bytes 1572896 | tf_op jit(solution)/shard_map/ppermute | solution.py:50
  102.7 3.5 %shard_map.63 = (bf16[3,128,2048]{2,1,0:T(8,128)(2,1)}, bf16[3,128,2048]{2,1,0:T(8,128)(2,1)}) custom-call(s32[256]{0:T(256)S(1)} %shard_map.56.table, bf16[4,128,2048]{2,1,0:T(8,128)(2,1)S(1)} %shard_map.55.refs_0_, bf16[4,128,2048]{2,1,0:T(8,128)(2,1)} %shard_map.57.refs_1_, bf16[4,128,2048]{2,1,0:T(8,128)(2,1)} %collective-permute-done.12.refs_2_, ...), custom_call_target="tpu_custom_call" | custom-call | bytes 1024 | tf_op jit(solution)/shard_map/pallas_call | solution.py:270
  106.3 2.7 %collective-permute-start.22 = (bf16[3,128,2048]{2,1,0:T(8,128)(2,1)}, bf16[3,128,2048]{2,1,0:T(8,128)(2,1)}, u32[]{:S(2)}, u32[]{:S(2)}) collective-permute-start(bf16[3,128,2048]{2,1,0:T(8,128)(2,1)} %get-tuple-element.208), channel_id=1, source_target_pairs={{0,96},{1,25},{2,98},{3,27},{4,100},{5,29},{6,102},{7,31},{8,104},... | collective-permute-start | bytes 4718600 | tf_op jit(solution)/shard_map/ppermute | solution.py:50
  109.1 10.5 %collective-permute-done.19.refs_10_.refs_5_ = bf16[3,128,2048]{2,1,0:T(8,128)(2,1)} collective-permute-done((bf16[3,128,2048]{2,1,0:T(8,128)(2,1)}, bf16[3,128,2048]{2,1,0:T(8,128)(2,1)}, u32[]{:S(2)}, u32[]{:S(2)}) %collective-permute-start.19) | collective-permute-done | bytes 1572896 | tf_op jit(solution)/shard_map/ppermute | solution.py:50
  119.6 3.9 %shard_map.61 = (bf16[3,128,2048]{2,1,0:T(8,128)(2,1)}, bf16[3,128,2048]{2,1,0:T(8,128)(2,1)}) custom-call(s32[256]{0:T(256)S(1)} %shard_map.56.table, bf16[4,128,2048]{2,1,0:T(8,128)(2,1)S(1)} %shard_map.55.refs_0_, bf16[4,128,2048]{2,1,0:T(8,128)(2,1)} %shard_map.57.refs_1_, bf16[4,128,2048]{2,1,0:T(8,128)(2,1)} %collective-permute-done.12.refs_2_, ...), custom_call_target="tpu_custom_call" | custom-call | bytes 1024 | tf_op jit(solution)/shard_map/pallas_call | solution.py:270
  123.6 2.7 %collective-permute-start.24 = (bf16[3,128,2048]{2,1,0:T(8,128)(2,1)}, bf16[3,128,2048]{2,1,0:T(8,128)(2,1)}, u32[]{:S(2)}, u32[]{:S(2)}) collective-permute-start(bf16[3,128,2048]{2,1,0:T(8,128)(2,1)} %get-tuple-element.212), channel_id=1, source_target_pairs={{0,96},{1,25},{2,98},{3,27},{4,100},{5,29},{6,102},{7,31},{8,104},... | collective-permute-start | bytes 4718600 | tf_op jit(solution)/shard_map/ppermute | solution.py:50
  128.2 12.7 %shard_map.62.refs_0_ = f32[1024,2048]{1,0:T(8,128)} custom-call(s32[256]{0:T(256)S(1)} %shard_map.56.table, bf16[8,16,2,128,128]{4,3,2,1,0:T(8,128)(2,1)} %bitcast.8, f32[1024,2048]{1,0:T(8,128)} %shard_map.58.refs_0_, bf16[4,128,2048]{2,1,0:T(8,128)(2,1)} %collective-permute-done.15.refs_6_.refs_1_, ...), custom_call_target="tpu_custom_call" | custom-call | bytes 1024 | tf_op jit(solution)/shard_map/pallas_call | solution.py:467
  140.9 8.2 %shard_map.64 = f32[1024,2048]{1,0:T(8,128)} custom-call(s32[256]{0:T(256)S(1)} %shard_map.56.table, bf16[8,16,2,128,128]{4,3,2,1,0:T(8,128)(2,1)} %bitcast.9, f32[1024,2048]{1,0:T(8,128)} %shard_map.62.refs_0_, bf16[3,128,2048]{2,1,0:T(8,128)(2,1)} %collective-permute-done.21.refs_1_, bf16[3,128,2048]{2,1,0:T(8,128)(2,1)} %collective-permute-done.22.refs_2_), custom_call_target="tpu_custom_call" | custom-call | bytes 1024 | tf_op jit(solution)/shard_map/pallas_call | solution.py:467
  149.1 4.2 %collective-permute-done.23 = bf16[3,128,2048]{2,1,0:T(8,128)(2,1)} collective-permute-done((bf16[3,128,2048]{2,1,0:T(8,128)(2,1)}, bf16[3,128,2048]{2,1,0:T(8,128)(2,1)}, u32[]{:S(2)}, u32[]{:S(2)}) %collective-permute-start.23) | collective-permute-done | bytes 1572896 | tf_op jit(solution)/shard_map/ppermute | solution.py:50
  153.3 9.6 %conditional.1 = (f32[16,16]{1,0:T(8,128)S(1)}) conditional(s32[]{:T(128)} %bitcast.2, (s32[256]{0:T(256)S(1)}, bf16[8,16,2,128,128]{4,3,2,1,0:T(8,128)(2,1)}, f32[1024,2048]{1,0:T(8,128)}, bf16[256,256]{1,0:T(8,128)(2,1)S(1)}, bf16[4,128,2048]{2,1,0:T(8,128)(2,1)S(1)}, /*index=5*/bf16[4,128,2048]{2,1,0:T(8,128)(2,1)}, ...), branch_computations={%region_0.0_spmd, %region_1.0_spmd, %region_2.0_spmd} | conditional | bytes 37752032 | solution.py:559
  153.3 9.4 %branch_0_fun.1 = f32[16,16]{1,0:T(8,128)S(1)} custom-call(s32[256]{0:T(256)S(1)} %get-tuple-element.104.table, bf16[8,16,2,128,128]{4,3,2,1,0:T(8,128)(2,1)} %get-tuple-element.106.own_c, f32[1024,2048]{1,0:T(8,128)} %get-tuple-element.107.before, bf16[256,256]{1,0:T(8,128)(2,1)S(1)} %get-tuple-element.108.turn, ...), custom_call_target="tpu_custom_call" | custom-call | bytes 1024 | tf_op jit(solution)/shard_map/cond/branch_0_fun/pallas_call | solution.py:467
  163.0 20.0 %all_to_all.9 = f32[128,1,2]{2,1,0:T(1,128)S(1)} all-to-all(f32[128,1,2]{2,1,0:T(1,128)S(1)} %bitcast.13), channel_id=1, replica_groups=mesh['ao'=16,'aux'=8] {'ao','aux'}, dimensions={0} | all-to-all | bytes 2048 | tf_op jit(solution)/shard_map/all_to_all | solution.py:561
  (37 shorter events, 4.3 us)
Async XLA Ops:
  0.0 2.6 %copy-start.5 = (s32[1,16,2]{1,2,0:T(2,128)S(1)}, s32[1,16,2]{1,2,0:T(2,128)}, u32[]{:S(2)}) copy-start(s32[1,16,2]{1,2,0:T(2,128)} %param.9) | copy-start | bytes 388
  0.0 2.8 %copy-start.6 = (s32[1,16]{1,0:T(1,128)S(1)}, s32[1,16]{1,0:T(1,128)}, u32[]{:S(2)}) copy-start(s32[1,16]{1,0:T(1,128)} %param.10) | copy-start | bytes 196
  2.8 5.8 %collective-permute-start.6 = (s32[1,48]{1,0:T(1,128)S(1)}, s32[1,48]{1,0:T(1,128)S(1)}, u32[]{:S(2)}, u32[]{:S(2)}) collective-permute-start(s32[1,48]{1,0:T(1,128)S(1)} %pad_add_fusion.4), channel_id=1, source_target_pairs={{0,32},{1,9},{2,34},{3,11},{4,36},{5,13},{6,38},{7,15},{8,40},{9,1... | collective-permute-start | bytes 584 | tf_op jit(solution)/shard_map/ppermute | solution.py:50
  4.9 34.0 %collective-permute-start.11 = (bf16[4,128,2048]{2,1,0:T(8,128)(2,1)S(1)}, bf16[4,128,2048]{2,1,0:T(8,128)(2,1)}, u32[]{:S(2)}, u32[]{:S(2)}) collective-permute-start(bf16[4,128,2048]{2,1,0:T(8,128)(2,1)S(1)} %shard_map.55.refs_0_), channel_id=1, source_target_pairs={{0,8},{1,33},{2,10},{3,35},{4,12},{5,37},{6,14},{7,39},{8,16},{9,4... | collective-permute-start | bytes 6291464 | tf_op jit(solution)/shard_map/ppermute | solution.py:46
  6.5 32.4 %collective-permute-start.12 = (bf16[4,128,2048]{2,1,0:T(8,128)(2,1)S(1)}, bf16[4,128,2048]{2,1,0:T(8,128)(2,1)}, u32[]{:S(2)}, u32[]{:S(2)}) collective-permute-start(bf16[4,128,2048]{2,1,0:T(8,128)(2,1)S(1)} %shard_map.55.refs_0_), channel_id=1, source_target_pairs={{0,24},{1,97},{2,26},{3,99},{4,28},{5,101},{6,30},{7,103},{8,0},{9... | collective-permute-start | bytes 6291464 | tf_op jit(solution)/shard_map/ppermute | solution.py:46
  12.6 41.9 %collective-permute-start.13 = (bf16[4,128,2048]{2,1,0:T(8,128)(2,1)}, bf16[4,128,2048]{2,1,0:T(8,128)(2,1)}, u32[]{:S(2)}, u32[]{:S(2)}) collective-permute-start(bf16[4,128,2048]{2,1,0:T(8,128)(2,1)} %shard_map.57.refs_1_), channel_id=1, source_target_pairs={{0,24},{1,97},{2,26},{3,99},{4,28},{5,101},{6,30},{7,103},{8,0},{9... | collective-permute-start | bytes 6291464 | tf_op jit(solution)/shard_map/ppermute | solution.py:46
  15.0 4.0 %collective-permute-start.7 = (s32[2,48]{1,0:T(2,128)S(1)}, s32[2,48]{1,0:T(2,128)S(1)}, u32[]{:S(2)}, u32[]{:S(2)}) collective-permute-start(s32[2,48]{1,0:T(2,128)S(1)} %pad_add_fusion.3), channel_id=1, source_target_pairs={{0,64},{1,17},{2,66},{3,19},{4,68},{5,21},{6,70},{7,23},{8,72},{9,... | collective-permute-start | bytes 1160 | tf_op jit(solution)/shard_map/ppermute | solution.py:50
  19.0 3.7 %collective-permute-start.8 = (s32[4,48]{1,0:T(4,128)S(1)}, s32[4,48]{1,0:T(4,128)S(1)}, u32[]{:S(2)}, u32[]{:S(2)}) collective-permute-start(s32[4,48]{1,0:T(4,128)S(1)} %pad_add_fusion.2), channel_id=1, source_target_pairs={{0,1},{1,0},{2,3},{3,2},{4,5},{5,4},{6,7},{7,6},{8,9},{9,8},{10,11... | collective-permute-start | bytes 2312 | tf_op jit(solution)/shard_map/ppermute | solution.py:506
  22.7 4.1 %collective-permute-start.9 = (s32[4,48]{1,0:T(4,128)S(1)}, s32[4,48]{1,0:T(4,128)S(1)}, u32[]{:S(2)}, u32[]{:S(2)}) collective-permute-start(s32[4,48]{1,0:T(4,128)S(1)} %collective-permute-done.8), channel_id=1, source_target_pairs={{0,32},{1,9},{2,34},{3,11},{4,36},{5,13},{6,38},{7,15},{8,40},{9,1... | collective-permute-start | bytes 2312 | tf_op jit(solution)/shard_map/ppermute | solution.py:50
  26.8 4.1 %collective-permute-start.10 = (s32[8,48]{1,0:T(8,128)S(1)}, s32[8,48]{1,0:T(8,128)S(1)}, u32[]{:S(2)}, u32[]{:S(2)}) collective-permute-start(s32[8,48]{1,0:T(8,128)S(1)} %pad_add_fusion.1), channel_id=1, source_target_pairs={{0,64},{1,17},{2,66},{3,19},{4,68},{5,21},{6,70},{7,23},{8,72},{9,... | collective-permute-start | bytes 4616 | tf_op jit(solution)/shard_map/ppermute | solution.py:50
  27.6 30.1 %collective-permute-start.14 = (bf16[4,128,2048]{2,1,0:T(8,128)(2,1)}, bf16[4,128,2048]{2,1,0:T(8,128)(2,1)}, u32[]{:S(2)}, u32[]{:S(2)}) collective-permute-start(bf16[4,128,2048]{2,1,0:T(8,128)(2,1)} %shard_map.57.refs_1_), channel_id=1, source_target_pairs={{0,8},{1,33},{2,10},{3,35},{4,12},{5,37},{6,14},{7,39},{8,16},{9,4... | collective-permute-start | bytes 6291464 | tf_op jit(solution)/shard_map/ppermute | solution.py:46
  39.0 38.5 %collective-permute-start.15 = (bf16[4,128,2048]{2,1,0:T(8,128)(2,1)}, bf16[4,128,2048]{2,1,0:T(8,128)(2,1)}, u32[]{:S(2)}, u32[]{:S(2)}) collective-permute-start(bf16[4,128,2048]{2,1,0:T(8,128)(2,1)} %collective-permute-done.11.refs_4_), channel_id=1, source_target_pairs={{0,8},{1,33},{2,10},{3,35},{4,12},{5,37},{6,14},{7,39},{8,16},{9,4... | collective-permute-start | bytes 6291464 | tf_op jit(solution)/shard_map/ppermute | solution.py:46
  54.5 29.8 %collective-permute-start.16 = (bf16[4,128,2048]{2,1,0:T(8,128)(2,1)}, bf16[4,128,2048]{2,1,0:T(8,128)(2,1)}, u32[]{:S(2)}, u32[]{:S(2)}) collective-permute-start(bf16[4,128,2048]{2,1,0:T(8,128)(2,1)} %collective-permute-done.13.refs_3_), channel_id=1, source_target_pairs={{0,24},{1,97},{2,26},{3,99},{4,28},{5,101},{6,30},{7,103},{8,0},{9... | collective-permute-start | bytes 6291464 | tf_op jit(solution)/shard_map/ppermute | solution.py:46
  81.6 21.2 %collective-permute-start.17 = (bf16[3,128,2048]{2,1,0:T(8,128)(2,1)}, bf16[3,128,2048]{2,1,0:T(8,128)(2,1)}, u32[]{:S(2)}, u32[]{:S(2)}) collective-permute-start(bf16[3,128,2048]{2,1,0:T(8,128)(2,1)} %get-tuple-element.195), channel_id=1, source_target_pairs={{0,32},{1,9},{2,34},{3,11},{4,36},{5,13},{6,38},{7,15},{8,40},{9,1... | collective-permute-start | bytes 4718600 | tf_op jit(solution)/shard_map/ppermute | solution.py:50
  81.8 20.9 %collective-permute-start.18 = (bf16[3,128,2048]{2,1,0:T(8,128)(2,1)}, bf16[3,128,2048]{2,1,0:T(8,128)(2,1)}, u32[]{:S(2)}, u32[]{:S(2)}) collective-permute-start(bf16[3,128,2048]{2,1,0:T(8,128)(2,1)} %get-tuple-element.196), channel_id=1, source_target_pairs={{0,96},{1,25},{2,98},{3,27},{4,100},{5,29},{6,102},{7,31},{8,104},... | collective-permute-start | bytes 4718600 | tf_op jit(solution)/shard_map/ppermute | solution.py:50
  87.8 31.8 %collective-permute-start.19 = (bf16[3,128,2048]{2,1,0:T(8,128)(2,1)}, bf16[3,128,2048]{2,1,0:T(8,128)(2,1)}, u32[]{:S(2)}, u32[]{:S(2)}) collective-permute-start(bf16[3,128,2048]{2,1,0:T(8,128)(2,1)} %get-tuple-element.199), channel_id=1, source_target_pairs={{0,32},{1,9},{2,34},{3,11},{4,36},{5,13},{6,38},{7,15},{8,40},{9,1... | collective-permute-start | bytes 4718600 | tf_op jit(solution)/shard_map/ppermute | solution.py:50
  87.8 31.8 %collective-permute-start.20 = (bf16[3,128,2048]{2,1,0:T(8,128)(2,1)}, bf16[3,128,2048]{2,1,0:T(8,128)(2,1)}, u32[]{:S(2)}, u32[]{:S(2)}) collective-permute-start(bf16[3,128,2048]{2,1,0:T(8,128)(2,1)} %get-tuple-element.200), channel_id=1, source_target_pairs={{0,96},{1,25},{2,98},{3,27},{4,100},{5,29},{6,102},{7,31},{8,104},... | collective-permute-start | bytes 4718600 | tf_op jit(solution)/shard_map/ppermute | solution.py:50
  106.2 34.7 %collective-permute-start.21 = (bf16[3,128,2048]{2,1,0:T(8,128)(2,1)}, bf16[3,128,2048]{2,1,0:T(8,128)(2,1)}, u32[]{:S(2)}, u32[]{:S(2)}) collective-permute-start(bf16[3,128,2048]{2,1,0:T(8,128)(2,1)} %get-tuple-element.207), channel_id=1, source_target_pairs={{0,32},{1,9},{2,34},{3,11},{4,36},{5,13},{6,38},{7,15},{8,40},{9,1... | collective-permute-start | bytes 4718600 | tf_op jit(solution)/shard_map/ppermute | solution.py:50
  106.3 20.0 %copy-start.4 = (bf16[1,128,128]{2,1,0:T(8,128)(2,1)S(1)}, bf16[1,128,128]{2,1,0:T(8,128)(2,1)}, u32[]{:S(2)}) copy-start(bf16[1,128,128]{2,1,0:T(8,128)(2,1)} %param.12) | copy-start | bytes 98308
  106.3 34.6 %collective-permute-start.22 = (bf16[3,128,2048]{2,1,0:T(8,128)(2,1)}, bf16[3,128,2048]{2,1,0:T(8,128)(2,1)}, u32[]{:S(2)}, u32[]{:S(2)}) collective-permute-start(bf16[3,128,2048]{2,1,0:T(8,128)(2,1)} %get-tuple-element.208), channel_id=1, source_target_pairs={{0,96},{1,25},{2,98},{3,27},{4,100},{5,29},{6,102},{7,31},{8,104},... | collective-permute-start | bytes 4718600 | tf_op jit(solution)/shard_map/ppermute | solution.py:50
  123.5 29.8 %collective-permute-start.23 = (bf16[3,128,2048]{2,1,0:T(8,128)(2,1)}, bf16[3,128,2048]{2,1,0:T(8,128)(2,1)}, u32[]{:S(2)}, u32[]{:S(2)}) collective-permute-start(bf16[3,128,2048]{2,1,0:T(8,128)(2,1)} %get-tuple-element.211), channel_id=1, source_target_pairs={{0,32},{1,9},{2,34},{3,11},{4,36},{5,13},{6,38},{7,15},{8,40},{9,1... | collective-permute-start | bytes 4718600 | tf_op jit(solution)/shard_map/ppermute | solution.py:50
  123.6 29.7 %collective-permute-start.24 = (bf16[3,128,2048]{2,1,0:T(8,128)(2,1)}, bf16[3,128,2048]{2,1,0:T(8,128)(2,1)}, u32[]{:S(2)}, u32[]{:S(2)}) collective-permute-start(bf16[3,128,2048]{2,1,0:T(8,128)(2,1)} %get-tuple-element.212), channel_id=1, source_target_pairs={{0,96},{1,25},{2,98},{3,27},{4,100},{5,29},{6,102},{7,31},{8,104},... | collective-permute-start | bytes 4718600 | tf_op jit(solution)/shard_map/ppermute | solution.py:50

commit v2 on v1

--- a/solution.py
+++ b/solution.py
@@ -525,9 +525,11 @@
         )
 
     acc = add(None, (0, 1, 3), ())
-    table, acc, far[0] = lax.optimization_barrier((table, acc, far[0]))
+    table, acc = lax.optimization_barrier((table, acc))
     for q in range(ALWAYS):
         up, down = pack(q, table, tiles, came)
+        if q == 0:
+            up, down, table, far[0] = lax.optimization_barrier((up, down, table, far[0]))
         if q == ALWAYS - 1:
             up, down, acc = lax.optimization_barrier((up, down, acc))
             acc = add(acc, (FAR,), tuple(range(q - 1)))

time: 183 us -> 182 us (level)
  waiting for transfers between devices: 67.3 us -> 60.1 us
  Pallas kernels: 64.8 us -> 67.3 us
    ppermute x6, waiting for transfers between devices: 29.4 us -> 22.9 us  [across(): return lax.ppermute(array, AXES, shift(False, step))]
    pallas_call x4, Pallas kernels: 36.1 us -> 39.6 us  [run(): pl.pallas_call(kernel, out_shape=jax.ShapeDtypeStruct(shape, jnp.float32)...]
  transfers between devices with their start and end apart: 19 -> 19, of which waited for: 9 -> 13; matrix products, arithmetic and copies ran while one was open for 1% -> 1% of each run, Pallas kernels for 29% -> 31%
where the time goes in v2:
time: 182 us; the launch traced here: 181 us
  Pallas kernels  67.3 us (37%)
  waiting for transfers between devices  60.1 us (33%)
  starting transfers between devices  28.5 us (16%)
  blocking collectives  21 us (12%)
  other arithmetic  1.99 us (1%)
    pallas_call x4, Pallas kernels, run(): pl.pallas_call(kernel, out_shape=jax.ShapeDtypeStruct(shape, jnp.float32)...  39.6 us
    ppermute x12, waiting for transfers between devices, around(): return lax.ppermute(array, AXES, shift(True, step))  36.4 us
    ppermute x6, waiting for transfers between devices, across(): return lax.ppermute(array, AXES, shift(False, step))  22.9 us
    all_to_all x1, blocking collectives, per_device(): lax.all_to_all(partial.reshape(128, 2), AXES, split_axis=0, concat_axis=0...  21 us
    ppermute x12, starting transfers between devices, around(): return lax.ppermute(array, AXES, shift(True, step))  16.2 us
    pallas_call x4, Pallas kernels, pack(): pl.pallas_call(functools.partial(pack_kernel, step, held, relays), out_sh...  13.8 us
    ppermute x6, starting transfers between devices, across(): return lax.ppermute(array, AXES, shift(False, step))  9.44 us
    pallas_call x1, Pallas kernels, plan(): pl.pallas_call(plan_kernel, out_shape=jax.ShapeDtypeStruct((256,), jnp.in...  7.33 us
  transfers between devices with their start and end apart: 19, of which 13 were waited for; matrix products, arithmetic and copies ran while one was open for 1% of the time, Pallas kernels for 31%

profile of v2, /device:TPU:1, one launch (start us, length us, event | category | flops | bytes accessed | tf_op | source)
XLA Modules:
  0.0 181.4 jit_solution(17712532022572905138)
XLA Ops:
  0.0 2.6 %shard_map.55.refs_0_ = bf16[4,128,2048]{2,1,0:T(8,128)(2,1)S(1)} custom-call(bf16[1,1,8,128,16,128]{5,4,3,2,1,0:T(8,128)(2,1)} %tile.2), custom_call_target="tpu_custom_call" | custom-call | bytes 8388608 | tf_op jit(solution)/shard_map/pallas_call | solution.py:483
  2.8 2.0 %collective-permute-start.6 = (s32[1,48]{1,0:T(1,128)S(1)}, s32[1,48]{1,0:T(1,128)S(1)}, u32[]{:S(2)}, u32[]{:S(2)}) collective-permute-start(s32[1,48]{1,0:T(1,128)S(1)} %pad_add_fusion.4), channel_id=1, source_target_pairs={{0,32},{1,9},{2,34},{3,11},{4,36},{5,13},{6,38},{7,15},{8,40},{9,1... | collective-permute-start | bytes 584 | tf_op jit(solution)/shard_map/ppermute | solution.py:50
  4.9 1.6 collective-permute-start.11
  6.5 2.1 %collective-permute-start.12 = (bf16[4,128,2048]{2,1,0:T(8,128)(2,1)S(1)}, bf16[4,128,2048]{2,1,0:T(8,128)(2,1)}, u32[]{:S(2)}, u32[]{:S(2)}) collective-permute-start(bf16[4,128,2048]{2,1,0:T(8,128)(2,1)S(1)} %shard_map.55.refs_0_), channel_id=1, source_target_pairs={{0,24},{1,97},{2,26},{3,99},{4,28},{5,101},{6,30},{7,103},{8,0},{9... | collective-permute-start | bytes 6291464 | tf_op jit(solution)/shard_map/ppermute | solution.py:46
  8.7 4.0 %shard_map.57.refs_1_ = bf16[4,128,2048]{2,1,0:T(8,128)(2,1)} custom-call(bf16[1,1,8,128,16,128]{5,4,3,2,1,0:T(8,128)(2,1)} %tile.2), custom_call_target="tpu_custom_call" | custom-call | bytes 8388608 | tf_op jit(solution)/shard_map/pallas_call | solution.py:483
  12.6 2.4 %collective-permute-start.13 = (bf16[4,128,2048]{2,1,0:T(8,128)(2,1)}, bf16[4,128,2048]{2,1,0:T(8,128)(2,1)}, u32[]{:S(2)}, u32[]{:S(2)}) collective-permute-start(bf16[4,128,2048]{2,1,0:T(8,128)(2,1)} %shard_map.57.refs_1_), channel_id=1, source_target_pairs={{0,24},{1,97},{2,26},{3,99},{4,28},{5,101},{6,30},{7,103},{8,0},{9... | collective-permute-start | bytes 6291464 | tf_op jit(solution)/shard_map/ppermute | solution.py:46
  15.0 1.5 collective-permute-start.7
  16.5 2.5 %collective-permute-done.7 = s32[2,48]{1,0:T(2,128)S(1)} collective-permute-done((s32[2,48]{1,0:T(2,128)S(1)}, s32[2,48]{1,0:T(2,128)S(1)}, u32[]{:S(2)}, u32[]{:S(2)}) %collective-permute-start.7) | collective-permute-done | bytes 416 | tf_op jit(solution)/shard_map/ppermute | solution.py:50
  19.0 2.9 %collective-permute-start.8 = (s32[4,48]{1,0:T(4,128)S(1)}, s32[4,48]{1,0:T(4,128)S(1)}, u32[]{:S(2)}, u32[]{:S(2)}) collective-permute-start(s32[4,48]{1,0:T(4,128)S(1)} %pad_add_fusion.2), channel_id=1, source_target_pairs={{0,1},{1,0},{2,3},{3,2},{4,5},{5,4},{6,7},{7,6},{8,9},{9,8},{10,11... | collective-permute-start | bytes 2312 | tf_op jit(solution)/shard_map/ppermute | solution.py:506
  22.7 4.1 %collective-permute-done.9 = s32[4,48]{1,0:T(4,128)S(1)} collective-permute-done((s32[4,48]{1,0:T(4,128)S(1)}, s32[4,48]{1,0:T(4,128)S(1)}, u32[]{:S(2)}, u32[]{:S(2)}) %collective-permute-start.9) | collective-permute-done | bytes 800 | tf_op jit(solution)/shard_map/ppermute | solution.py:50
  27.6 3.4 %collective-permute-done.10 = s32[8,48]{1,0:T(8,128)S(1)} collective-permute-done((s32[8,48]{1,0:T(8,128)S(1)}, s32[8,48]{1,0:T(8,128)S(1)}, u32[]{:S(2)}, u32[]{:S(2)}) %collective-permute-start.10) | collective-permute-done | bytes 1568 | tf_op jit(solution)/shard_map/ppermute | solution.py:50
  31.6 7.3 %shard_map.56.table = s32[256]{0:T(256)S(1)} custom-call(s32[16,48]{1,0:T(8,128)} %pad_add_fusion.came, s32[2]{0:T(128)} %pad_add_fusion.5.where), custom_call_target="tpu_custom_call" | custom-call | tf_op jit(solution)/shard_map/pallas_call | solution.py:216
  39.1 15.4 %collective-permute-done.13.refs_3_ = bf16[4,128,2048]{2,1,0:T(8,128)(2,1)} collective-permute-done((bf16[4,128,2048]{2,1,0:T(8,128)(2,1)}, bf16[4,128,2048]{2,1,0:T(8,128)(2,1)}, u32[]{:S(2)}, u32[]{:S(2)}) %collective-permute-start.13) | collective-permute-done | bytes 2097184 | tf_op jit(solution)/shard_map/ppermute | solution.py:46
  54.5 3.2 %collective-permute-start.16 = (bf16[4,128,2048]{2,1,0:T(8,128)(2,1)}, bf16[4,128,2048]{2,1,0:T(8,128)(2,1)}, u32[]{:S(2)}, u32[]{:S(2)}) collective-permute-start(bf16[4,128,2048]{2,1,0:T(8,128)(2,1)} %collective-permute-done.13.refs_3_), channel_id=1, source_target_pairs={{0,24},{1,97},{2,26},{3,99},{4,28},{5,101},{6,30},{7,103},{8,0},{9... | collective-permute-start | bytes 6291464 | tf_op jit(solution)/shard_map/ppermute | solution.py:46
  57.7 9.6 %shard_map.58.refs_0_ = f32[1024,2048]{1,0:T(8,128)} custom-call(s32[256]{0:T(256)S(1)} %shard_map.56.table, bf16[8,16,2,128,128]{4,3,2,1,0:T(8,128)(2,1)} %bitcast.7, bf16[4,128,2048]{2,1,0:T(8,128)(2,1)S(1)} %shard_map.55.refs_0_, bf16[4,128,2048]{2,1,0:T(8,128)(2,1)} %shard_map.57.refs_1_, bf16[4,128,2048]{2,1,0:T(8,128)(2,1)} %collective-permute-done.12.refs_2_, ...), custom_call_target="tpu_custom_call" | custom-call | bytes 1024 | tf_op jit(solution)/shard_map/pallas_call | solution.py:467
  67.3 3.6 %shard_map.59 = (bf16[3,128,2048]{2,1,0:T(8,128)(2,1)}, bf16[3,128,2048]{2,1,0:T(8,128)(2,1)}) custom-call(s32[256]{0:T(256)S(1)} %shard_map.56.table, bf16[4,128,2048]{2,1,0:T(8,128)(2,1)S(1)} %shard_map.55.refs_0_, bf16[4,128,2048]{2,1,0:T(8,128)(2,1)} %shard_map.57.refs_1_, bf16[4,128,2048]{2,1,0:T(8,128)(2,1)} %collective-permute-done.12.refs_2_, ...), custom_call_target="tpu_custom_call" | custom-call | bytes 1024 | tf_op jit(solution)/shard_map/pallas_call | solution.py:270
  70.9 6.6 %collective-permute-done.15.refs_6_.refs_1_ = bf16[4,128,2048]{2,1,0:T(8,128)(2,1)} collective-permute-done((bf16[4,128,2048]{2,1,0:T(8,128)(2,1)}, bf16[4,128,2048]{2,1,0:T(8,128)(2,1)}, u32[]{:S(2)}, u32[]{:S(2)}) %collective-permute-start.15) | collective-permute-done | bytes 2097184 | tf_op jit(solution)/shard_map/ppermute | solution.py:46
  78.4 1.8 collective-permute-start.18
  81.0 3.4 %shard_map.60 = (bf16[3,128,2048]{2,1,0:T(8,128)(2,1)}, bf16[3,128,2048]{2,1,0:T(8,128)(2,1)}) custom-call(s32[256]{0:T(256)S(1)} %shard_map.56.table, bf16[4,128,2048]{2,1,0:T(8,128)(2,1)S(1)} %shard_map.55.refs_0_, bf16[4,128,2048]{2,1,0:T(8,128)(2,1)} %shard_map.57.refs_1_, bf16[4,128,2048]{2,1,0:T(8,128)(2,1)} %collective-permute-done.12.refs_2_, ...), custom_call_target="tpu_custom_call" | custom-call | bytes 1024 | tf_op jit(solution)/shard_map/pallas_call | solution.py:270
  85.4 1.8 collective-permute-start.20
  87.1 11.4 %collective-permute-done.17.refs_8_.refs_3_ = bf16[3,128,2048]{2,1,0:T(8,128)(2,1)} collective-permute-done((bf16[3,128,2048]{2,1,0:T(8,128)(2,1)}, bf16[3,128,2048]{2,1,0:T(8,128)(2,1)}, u32[]{:S(2)}, u32[]{:S(2)}) %collective-permute-start.17) | collective-permute-done | bytes 1572896 | tf_op jit(solution)/shard_map/ppermute | solution.py:50
  99.7 3.5 %shard_map.63 = (bf16[3,128,2048]{2,1,0:T(8,128)(2,1)}, bf16[3,128,2048]{2,1,0:T(8,128)(2,1)}) custom-call(s32[256]{0:T(256)S(1)} %shard_map.56.table, bf16[4,128,2048]{2,1,0:T(8,128)(2,1)S(1)} %shard_map.55.refs_0_, bf16[4,128,2048]{2,1,0:T(8,128)(2,1)} %shard_map.57.refs_1_, bf16[4,128,2048]{2,1,0:T(8,128)(2,1)} %collective-permute-done.12.refs_2_, ...), custom_call_target="tpu_custom_call" | custom-call | bytes 1024 | tf_op jit(solution)/shard_map/pallas_call | solution.py:270
  104.0 2.8 %collective-permute-start.22 = (bf16[3,128,2048]{2,1,0:T(8,128)(2,1)}, bf16[3,128,2048]{2,1,0:T(8,128)(2,1)}, u32[]{:S(2)}, u32[]{:S(2)}) collective-permute-start(bf16[3,128,2048]{2,1,0:T(8,128)(2,1)} %get-tuple-element.214), channel_id=1, source_target_pairs={{0,96},{1,25},{2,98},{3,27},{4,100},{5,29},{6,102},{7,31},{8,104},... | collective-permute-start | bytes 4718600 | tf_op jit(solution)/shard_map/ppermute | solution.py:50
  106.8 8.7 %collective-permute-done.19.refs_10_.refs_5_ = bf16[3,128,2048]{2,1,0:T(8,128)(2,1)} collective-permute-done((bf16[3,128,2048]{2,1,0:T(8,128)(2,1)}, bf16[3,128,2048]{2,1,0:T(8,128)(2,1)}, u32[]{:S(2)}, u32[]{:S(2)}) %collective-permute-start.19) | collective-permute-done | bytes 1572896 | tf_op jit(solution)/shard_map/ppermute | solution.py:50
  116.6 3.4 %shard_map.61 = (bf16[3,128,2048]{2,1,0:T(8,128)(2,1)}, bf16[3,128,2048]{2,1,0:T(8,128)(2,1)}) custom-call(s32[256]{0:T(256)S(1)} %shard_map.56.table, bf16[4,128,2048]{2,1,0:T(8,128)(2,1)S(1)} %shard_map.55.refs_0_, bf16[4,128,2048]{2,1,0:T(8,128)(2,1)} %shard_map.57.refs_1_, bf16[4,128,2048]{2,1,0:T(8,128)(2,1)} %collective-permute-done.12.refs_2_, ...), custom_call_target="tpu_custom_call" | custom-call | bytes 1024 | tf_op jit(solution)/shard_map/pallas_call | solution.py:270
  120.8 2.8 %collective-permute-start.24 = (bf16[3,128,2048]{2,1,0:T(8,128)(2,1)}, bf16[3,128,2048]{2,1,0:T(8,128)(2,1)}, u32[]{:S(2)}, u32[]{:S(2)}) collective-permute-start(bf16[3,128,2048]{2,1,0:T(8,128)(2,1)} %get-tuple-element.218), channel_id=1, source_target_pairs={{0,96},{1,25},{2,98},{3,27},{4,100},{5,29},{6,102},{7,31},{8,104},... | collective-permute-start | bytes 4718600 | tf_op jit(solution)/shard_map/ppermute | solution.py:50
  125.4 12.7 %shard_map.62.refs_0_ = f32[1024,2048]{1,0:T(8,128)} custom-call(s32[256]{0:T(256)S(1)} %shard_map.56.table, bf16[8,16,2,128,128]{4,3,2,1,0:T(8,128)(2,1)} %bitcast.8, f32[1024,2048]{1,0:T(8,128)} %shard_map.58.refs_0_, bf16[4,128,2048]{2,1,0:T(8,128)(2,1)} %collective-permute-done.15.refs_6_.refs_1_, ...), custom_call_target="tpu_custom_call" | custom-call | bytes 1024 | tf_op jit(solution)/shard_map/pallas_call | solution.py:467
  138.1 8.2 %shard_map.64 = f32[1024,2048]{1,0:T(8,128)} custom-call(s32[256]{0:T(256)S(1)} %shard_map.56.table, bf16[8,16,2,128,128]{4,3,2,1,0:T(8,128)(2,1)} %bitcast.9, f32[1024,2048]{1,0:T(8,128)} %shard_map.62.refs_0_, bf16[3,128,2048]{2,1,0:T(8,128)(2,1)} %collective-permute-done.21.refs_1_, bf16[3,128,2048]{2,1,0:T(8,128)(2,1)} %collective-permute-done.22.refs_2_), custom_call_target="tpu_custom_call" | custom-call | bytes 1024 | tf_op jit(solution)/shard_map/pallas_call | solution.py:467
  146.3 2.8 %collective-permute-done.23 = bf16[3,128,2048]{2,1,0:T(8,128)(2,1)} collective-permute-done((bf16[3,128,2048]{2,1,0:T(8,128)(2,1)}, bf16[3,128,2048]{2,1,0:T(8,128)(2,1)}, u32[]{:S(2)}, u32[]{:S(2)}) %collective-permute-start.23) | collective-permute-done | bytes 1572896 | tf_op jit(solution)/shard_map/ppermute | solution.py:50
  150.3 9.4 %conditional.1 = (f32[16,16]{1,0:T(8,128)S(1)}) conditional(s32[]{:T(128)} %bitcast.2, (s32[256]{0:T(256)S(1)}, bf16[8,16,2,128,128]{4,3,2,1,0:T(8,128)(2,1)}, f32[1024,2048]{1,0:T(8,128)}, bf16[256,256]{1,0:T(8,128)(2,1)S(1)}, bf16[4,128,2048]{2,1,0:T(8,128)(2,1)S(1)}, /*index=5*/bf16[4,128,2048]{2,1,0:T(8,128)(2,1)}, ...), branch_computations={%region_0.0_spmd, %region_1.0_spmd, %region_2.0_spmd} | conditional | bytes 37752032 | solution.py:561
  150.3 9.1 %branch_0_fun.1 = f32[16,16]{1,0:T(8,128)S(1)} custom-call(s32[256]{0:T(256)S(1)} %get-tuple-element.104.table, bf16[8,16,2,128,128]{4,3,2,1,0:T(8,128)(2,1)} %get-tuple-element.106.own_c, f32[1024,2048]{1,0:T(8,128)} %get-tuple-element.107.before, bf16[256,256]{1,0:T(8,128)(2,1)S(1)} %get-tuple-element.108.turn, ...), custom_call_target="tpu_custom_call" | custom-call | bytes 1024 | tf_op jit(solution)/shard_map/cond/branch_0_fun/pallas_call | solution.py:467
  159.7 21.0 %all_to_all.9 = f32[128,1,2]{2,1,0:T(1,128)S(1)} all-to-all(f32[128,1,2]{2,1,0:T(1,128)S(1)} %bitcast.13), channel_id=1, replica_groups=mesh['ao'=16,'aux'=8] {'ao','aux'}, dimensions={0} | all-to-all | bytes 2048 | tf_op jit(solution)/shard_map/all_to_all | solution.py:563
  (37 shorter events, 11.5 us)
Async XLA Ops:
  0.0 2.6 %copy-start.5 = (s32[1,16,2]{1,2,0:T(2,128)S(1)}, s32[1,16,2]{1,2,0:T(2,128)}, u32[]{:S(2)}) copy-start(s32[1,16,2]{1,2,0:T(2,128)} %param.9) | copy-start | bytes 388
  0.0 2.8 %copy-start.6 = (s32[1,16]{1,0:T(1,128)S(1)}, s32[1,16]{1,0:T(1,128)}, u32[]{:S(2)}) copy-start(s32[1,16]{1,0:T(1,128)} %param.10) | copy-start | bytes 196
  2.8 5.8 %collective-permute-start.6 = (s32[1,48]{1,0:T(1,128)S(1)}, s32[1,48]{1,0:T(1,128)S(1)}, u32[]{:S(2)}, u32[]{:S(2)}) collective-permute-start(s32[1,48]{1,0:T(1,128)S(1)} %pad_add_fusion.4), channel_id=1, source_target_pairs={{0,32},{1,9},{2,34},{3,11},{4,36},{5,13},{6,38},{7,15},{8,40},{9,1... | collective-permute-start | bytes 584 | tf_op jit(solution)/shard_map/ppermute | solution.py:50
  4.9 34.0 %collective-permute-start.11 = (bf16[4,128,2048]{2,1,0:T(8,128)(2,1)S(1)}, bf16[4,128,2048]{2,1,0:T(8,128)(2,1)}, u32[]{:S(2)}, u32[]{:S(2)}) collective-permute-start(bf16[4,128,2048]{2,1,0:T(8,128)(2,1)S(1)} %shard_map.55.refs_0_), channel_id=1, source_target_pairs={{0,8},{1,33},{2,10},{3,35},{4,12},{5,37},{6,14},{7,39},{8,16},{9,4... | collective-permute-start | bytes 6291464 | tf_op jit(solution)/shard_map/ppermute | solution.py:46
  6.5 32.4 %collective-permute-start.12 = (bf16[4,128,2048]{2,1,0:T(8,128)(2,1)S(1)}, bf16[4,128,2048]{2,1,0:T(8,128)(2,1)}, u32[]{:S(2)}, u32[]{:S(2)}) collective-permute-start(bf16[4,128,2048]{2,1,0:T(8,128)(2,1)S(1)} %shard_map.55.refs_0_), channel_id=1, source_target_pairs={{0,24},{1,97},{2,26},{3,99},{4,28},{5,101},{6,30},{7,103},{8,0},{9... | collective-permute-start | bytes 6291464 | tf_op jit(solution)/shard_map/ppermute | solution.py:46
  12.6 41.9 %collective-permute-start.13 = (bf16[4,128,2048]{2,1,0:T(8,128)(2,1)}, bf16[4,128,2048]{2,1,0:T(8,128)(2,1)}, u32[]{:S(2)}, u32[]{:S(2)}) collective-permute-start(bf16[4,128,2048]{2,1,0:T(8,128)(2,1)} %shard_map.57.refs_1_), channel_id=1, source_target_pairs={{0,24},{1,97},{2,26},{3,99},{4,28},{5,101},{6,30},{7,103},{8,0},{9... | collective-permute-start | bytes 6291464 | tf_op jit(solution)/shard_map/ppermute | solution.py:46
  15.0 4.0 %collective-permute-start.7 = (s32[2,48]{1,0:T(2,128)S(1)}, s32[2,48]{1,0:T(2,128)S(1)}, u32[]{:S(2)}, u32[]{:S(2)}) collective-permute-start(s32[2,48]{1,0:T(2,128)S(1)} %pad_add_fusion.3), channel_id=1, source_target_pairs={{0,64},{1,17},{2,66},{3,19},{4,68},{5,21},{6,70},{7,23},{8,72},{9,... | collective-permute-start | bytes 1160 | tf_op jit(solution)/shard_map/ppermute | solution.py:50
  19.0 3.7 %collective-permute-start.8 = (s32[4,48]{1,0:T(4,128)S(1)}, s32[4,48]{1,0:T(4,128)S(1)}, u32[]{:S(2)}, u32[]{:S(2)}) collective-permute-start(s32[4,48]{1,0:T(4,128)S(1)} %pad_add_fusion.2), channel_id=1, source_target_pairs={{0,1},{1,0},{2,3},{3,2},{4,5},{5,4},{6,7},{7,6},{8,9},{9,8},{10,11... | collective-permute-start | bytes 2312 | tf_op jit(solution)/shard_map/ppermute | solution.py:506
  22.7 4.1 %collective-permute-start.9 = (s32[4,48]{1,0:T(4,128)S(1)}, s32[4,48]{1,0:T(4,128)S(1)}, u32[]{:S(2)}, u32[]{:S(2)}) collective-permute-start(s32[4,48]{1,0:T(4,128)S(1)} %collective-permute-done.8), channel_id=1, source_target_pairs={{0,32},{1,9},{2,34},{3,11},{4,36},{5,13},{6,38},{7,15},{8,40},{9,1... | collective-permute-start | bytes 2312 | tf_op jit(solution)/shard_map/ppermute | solution.py:50
  26.8 4.1 %collective-permute-start.10 = (s32[8,48]{1,0:T(8,128)S(1)}, s32[8,48]{1,0:T(8,128)S(1)}, u32[]{:S(2)}, u32[]{:S(2)}) collective-permute-start(s32[8,48]{1,0:T(8,128)S(1)} %pad_add_fusion.1), channel_id=1, source_target_pairs={{0,64},{1,17},{2,66},{3,19},{4,68},{5,21},{6,70},{7,23},{8,72},{9,... | collective-permute-start | bytes 4616 | tf_op jit(solution)/shard_map/ppermute | solution.py:50
  27.6 30.1 %collective-permute-start.14 = (bf16[4,128,2048]{2,1,0:T(8,128)(2,1)}, bf16[4,128,2048]{2,1,0:T(8,128)(2,1)}, u32[]{:S(2)}, u32[]{:S(2)}) collective-permute-start(bf16[4,128,2048]{2,1,0:T(8,128)(2,1)} %shard_map.57.refs_1_), channel_id=1, source_target_pairs={{0,8},{1,33},{2,10},{3,35},{4,12},{5,37},{6,14},{7,39},{8,16},{9,4... | collective-permute-start | bytes 6291464 | tf_op jit(solution)/shard_map/ppermute | solution.py:46
  38.9 38.5 %collective-permute-start.15 = (bf16[4,128,2048]{2,1,0:T(8,128)(2,1)}, bf16[4,128,2048]{2,1,0:T(8,128)(2,1)}, u32[]{:S(2)}, u32[]{:S(2)}) collective-permute-start(bf16[4,128,2048]{2,1,0:T(8,128)(2,1)} %collective-permute-done.11.refs_4_), channel_id=1, source_target_pairs={{0,8},{1,33},{2,10},{3,35},{4,12},{5,37},{6,14},{7,39},{8,16},{9,4... | collective-permute-start | bytes 6291464 | tf_op jit(solution)/shard_map/ppermute | solution.py:46
  54.5 26.5 %collective-permute-start.16 = (bf16[4,128,2048]{2,1,0:T(8,128)(2,1)}, bf16[4,128,2048]{2,1,0:T(8,128)(2,1)}, u32[]{:S(2)}, u32[]{:S(2)}) collective-permute-start(bf16[4,128,2048]{2,1,0:T(8,128)(2,1)} %collective-permute-done.13.refs_3_), channel_id=1, source_target_pairs={{0,24},{1,97},{2,26},{3,99},{4,28},{5,101},{6,30},{7,103},{8,0},{9... | collective-permute-start | bytes 6291464 | tf_op jit(solution)/shard_map/ppermute | solution.py:46
  77.5 21.1 %collective-permute-start.17 = (bf16[3,128,2048]{2,1,0:T(8,128)(2,1)}, bf16[3,128,2048]{2,1,0:T(8,128)(2,1)}, u32[]{:S(2)}, u32[]{:S(2)}) collective-permute-start(bf16[3,128,2048]{2,1,0:T(8,128)(2,1)} %get-tuple-element.201), channel_id=1, source_target_pairs={{0,32},{1,9},{2,34},{3,11},{4,36},{5,13},{6,38},{7,15},{8,40},{9,1... | collective-permute-start | bytes 4718600 | tf_op jit(solution)/shard_map/ppermute | solution.py:50
  78.4 21.3 %collective-permute-start.18 = (bf16[3,128,2048]{2,1,0:T(8,128)(2,1)}, bf16[3,128,2048]{2,1,0:T(8,128)(2,1)}, u32[]{:S(2)}, u32[]{:S(2)}) collective-permute-start(bf16[3,128,2048]{2,1,0:T(8,128)(2,1)} %get-tuple-element.202), channel_id=1, source_target_pairs={{0,96},{1,25},{2,98},{3,27},{4,100},{5,29},{6,102},{7,31},{8,104},... | collective-permute-start | bytes 4718600 | tf_op jit(solution)/shard_map/ppermute | solution.py:50
  84.4 31.0 %collective-permute-start.19 = (bf16[3,128,2048]{2,1,0:T(8,128)(2,1)}, bf16[3,128,2048]{2,1,0:T(8,128)(2,1)}, u32[]{:S(2)}, u32[]{:S(2)}) collective-permute-start(bf16[3,128,2048]{2,1,0:T(8,128)(2,1)} %get-tuple-element.205), channel_id=1, source_target_pairs={{0,32},{1,9},{2,34},{3,11},{4,36},{5,13},{6,38},{7,15},{8,40},{9,1... | collective-permute-start | bytes 4718600 | tf_op jit(solution)/shard_map/ppermute | solution.py:50
  85.4 31.2 %collective-permute-start.20 = (bf16[3,128,2048]{2,1,0:T(8,128)(2,1)}, bf16[3,128,2048]{2,1,0:T(8,128)(2,1)}, u32[]{:S(2)}, u32[]{:S(2)}) collective-permute-start(bf16[3,128,2048]{2,1,0:T(8,128)(2,1)} %get-tuple-element.206), channel_id=1, source_target_pairs={{0,96},{1,25},{2,98},{3,27},{4,100},{5,29},{6,102},{7,31},{8,104},... | collective-permute-start | bytes 4718600 | tf_op jit(solution)/shard_map/ppermute | solution.py:50
  103.2 34.9 %collective-permute-start.21 = (bf16[3,128,2048]{2,1,0:T(8,128)(2,1)}, bf16[3,128,2048]{2,1,0:T(8,128)(2,1)}, u32[]{:S(2)}, u32[]{:S(2)}) collective-permute-start(bf16[3,128,2048]{2,1,0:T(8,128)(2,1)} %get-tuple-element.213), channel_id=1, source_target_pairs={{0,32},{1,9},{2,34},{3,11},{4,36},{5,13},{6,38},{7,15},{8,40},{9,1... | collective-permute-start | bytes 4718600 | tf_op jit(solution)/shard_map/ppermute | solution.py:50
  104.0 19.6 %copy-start.4 = (bf16[1,128,128]{2,1,0:T(8,128)(2,1)S(1)}, bf16[1,128,128]{2,1,0:T(8,128)(2,1)}, u32[]{:S(2)}) copy-start(bf16[1,128,128]{2,1,0:T(8,128)(2,1)} %param.12) | copy-start | bytes 98308
  104.0 34.1 %collective-permute-start.22 = (bf16[3,128,2048]{2,1,0:T(8,128)(2,1)}, bf16[3,128,2048]{2,1,0:T(8,128)(2,1)}, u32[]{:S(2)}, u32[]{:S(2)}) collective-permute-start(bf16[3,128,2048]{2,1,0:T(8,128)(2,1)} %get-tuple-element.214), channel_id=1, source_target_pairs={{0,96},{1,25},{2,98},{3,27},{4,100},{5,29},{6,102},{7,31},{8,104},... | collective-permute-start | bytes 4718600 | tf_op jit(solution)/shard_map/ppermute | solution.py:50
  120.0 29.2 %collective-permute-start.23 = (bf16[3,128,2048]{2,1,0:T(8,128)(2,1)}, bf16[3,128,2048]{2,1,0:T(8,128)(2,1)}, u32[]{:S(2)}, u32[]{:S(2)}) collective-permute-start(bf16[3,128,2048]{2,1,0:T(8,128)(2,1)} %get-tuple-element.217), channel_id=1, source_target_pairs={{0,32},{1,9},{2,34},{3,11},{4,36},{5,13},{6,38},{7,15},{8,40},{9,1... | collective-permute-start | bytes 4718600 | tf_op jit(solution)/shard_map/ppermute | solution.py:50
  120.8 29.5 %collective-permute-start.24 = (bf16[3,128,2048]{2,1,0:T(8,128)(2,1)}, bf16[3,128,2048]{2,1,0:T(8,128)(2,1)}, u32[]{:S(2)}, u32[]{:S(2)}) collective-permute-start(bf16[3,128,2048]{2,1,0:T(8,128)(2,1)} %get-tuple-element.218), channel_id=1, source_target_pairs={{0,96},{1,25},{2,98},{3,27},{4,100},{5,29},{6,102},{7,31},{8,104},... | collective-permute-start | bytes 4718600 | tf_op jit(solution)/shard_map/ppermute | solution.py:50

commit v3 on v2

--- a/solution.py
+++ b/solution.py
@@ -378,13 +378,14 @@
 def last_kernel(steps, table, own_c, before, turn, first, second, *refs):
     came = refs[:2 * len(steps)]
     out, left, right, acc, rows, part, mixed, total, sems = refs[2 * len(steps):]
-    n = gather(own_c, left, right, sems, from_steps(table, steps, came))
     fetches = []
     for j in range(PARTS):
         cols = pl.ds(j * WIDE // PARTS, WIDE // PARTS)
-        copy = pltpu.make_async_copy(before.at[:, cols], acc.at[:, cols], sems.at[2 + j])
+        fetches.append(pltpu.make_async_copy(before.at[:, cols], acc.at[:, cols], sems.at[2 + j]))
+    fetches[0].start()
+    n = gather(own_c, left, right, sems, from_steps(table, steps, came))
+    for copy in fetches[1:]:
         copy.start()
-        fetches.append(copy)
     own = []
     for c, chunk in enumerate((first, second)):
         copy = pltpu.make_async_copy(chunk, rows.at[pl.ds(c * PER, PER)], sems.at[2 + PARTS + c])

time: 182 us -> 181 us (level)
  waiting for transfers between devices: 60.1 us -> 65.1 us
  Pallas kernels: 67.3 us -> 63 us
    pallas_call x4, Pallas kernels: 39.6 us -> 35 us  [run(): pl.pallas_call(kernel, out_shape=jax.ShapeDtypeStruct(shape, jnp.float32)...]
    ppermute x6, waiting for transfers between devices: 22.9 us -> 25.5 us  [across(): return lax.ppermute(array, AXES, shift(False, step))]
    ppermute x12, waiting for transfers between devices: 36.4 us -> 38.7 us  [around(): return lax.ppermute(array, AXES, shift(True, step))]
  transfers between devices with their start and end apart: 19 -> 19, of which waited for: 13 -> 13; matrix products, arithmetic and copies ran while one was open for 1% -> 1% of each run, Pallas kernels for 31% -> 28%
where the time goes in v3:
time: 181 us
  waiting for transfers between devices  65.1 us (36%)
  Pallas kernels  63 us (35%)
  starting transfers between devices  28 us (15%)
  blocking collectives  20.9 us (12%)
  other arithmetic  1.99 us (1%)
    ppermute x12, waiting for transfers between devices, around(): return lax.ppermute(array, AXES, shift(True, step))  38.7 us
    pallas_call x4, Pallas kernels, run(): pl.pallas_call(kernel, out_shape=jax.ShapeDtypeStruct(shape, jnp.float32)...  35 us
    ppermute x6, waiting for transfers between devices, across(): return lax.ppermute(array, AXES, shift(False, step))  25.5 us
    all_to_all x1, blocking collectives, per_device(): lax.all_to_all(partial.reshape(128, 2), AXES, split_axis=0, concat_axis=0...  20.9 us
    ppermute x12, starting transfers between devices, around(): return lax.ppermute(array, AXES, shift(True, step))  15.7 us
    pallas_call x4, Pallas kernels, pack(): pl.pallas_call(functools.partial(pack_kernel, step, held, relays), out_sh...  14.1 us
    ppermute x6, starting transfers between devices, across(): return lax.ppermute(array, AXES, shift(False, step))  9.4 us
    pallas_call x1, Pallas kernels, plan(): pl.pallas_call(plan_kernel, out_shape=jax.ShapeDtypeStruct((256,), jnp.in...  7.38 us
  transfers between devices with their start and end apart: 19, of which 13 were waited for; matrix products, arithmetic and copies ran while one was open for 1% of the time, Pallas kernels for 28%

profile of v3, /device:TPU:1, one launch (start us, length us, event | category | flops | bytes accessed | tf_op | source)
XLA Modules:
  0.0 181.4 jit_solution(11203957584569584409)
XLA Ops:
  0.0 2.6 %shard_map.55.refs_0_ = bf16[4,128,2048]{2,1,0:T(8,128)(2,1)S(1)} custom-call(bf16[1,1,8,128,16,128]{5,4,3,2,1,0:T(8,128)(2,1)} %tile.2), custom_call_target="tpu_custom_call" | custom-call | bytes 8388608 | tf_op jit(solution)/shard_map/pallas_call | solution.py:484
  2.8 2.0 %collective-permute-start.6 = (s32[1,48]{1,0:T(1,128)S(1)}, s32[1,48]{1,0:T(1,128)S(1)}, u32[]{:S(2)}, u32[]{:S(2)}) collective-permute-start(s32[1,48]{1,0:T(1,128)S(1)} %pad_add_fusion.4), channel_id=1, source_target_pairs={{0,32},{1,9},{2,34},{3,11},{4,36},{5,13},{6,38},{7,15},{8,40},{9,1... | collective-permute-start | bytes 584 | tf_op jit(solution)/shard_map/ppermute | solution.py:50
  4.9 1.6 collective-permute-start.11
  6.5 2.1 %collective-permute-start.12 = (bf16[4,128,2048]{2,1,0:T(8,128)(2,1)S(1)}, bf16[4,128,2048]{2,1,0:T(8,128)(2,1)}, u32[]{:S(2)}, u32[]{:S(2)}) collective-permute-start(bf16[4,128,2048]{2,1,0:T(8,128)(2,1)S(1)} %shard_map.55.refs_0_), channel_id=1, source_target_pairs={{0,24},{1,97},{2,26},{3,99},{4,28},{5,101},{6,30},{7,103},{8,0},{9... | collective-permute-start | bytes 6291464 | tf_op jit(solution)/shard_map/ppermute | solution.py:46
  8.7 4.0 %shard_map.57.refs_1_ = bf16[4,128,2048]{2,1,0:T(8,128)(2,1)} custom-call(bf16[1,1,8,128,16,128]{5,4,3,2,1,0:T(8,128)(2,1)} %tile.2), custom_call_target="tpu_custom_call" | custom-call | bytes 8388608 | tf_op jit(solution)/shard_map/pallas_call | solution.py:484
  12.6 2.4 %collective-permute-start.13 = (bf16[4,128,2048]{2,1,0:T(8,128)(2,1)}, bf16[4,128,2048]{2,1,0:T(8,128)(2,1)}, u32[]{:S(2)}, u32[]{:S(2)}) collective-permute-start(bf16[4,128,2048]{2,1,0:T(8,128)(2,1)} %shard_map.57.refs_1_), channel_id=1, source_target_pairs={{0,24},{1,97},{2,26},{3,99},{4,28},{5,101},{6,30},{7,103},{8,0},{9... | collective-permute-start | bytes 6291464 | tf_op jit(solution)/shard_map/ppermute | solution.py:46
  15.0 1.5 collective-permute-start.7
  16.5 2.5 %collective-permute-done.7 = s32[2,48]{1,0:T(2,128)S(1)} collective-permute-done((s32[2,48]{1,0:T(2,128)S(1)}, s32[2,48]{1,0:T(2,128)S(1)}, u32[]{:S(2)}, u32[]{:S(2)}) %collective-permute-start.7) | collective-permute-done | bytes 416 | tf_op jit(solution)/shard_map/ppermute | solution.py:50
  19.0 2.9 %collective-permute-start.8 = (s32[4,48]{1,0:T(4,128)S(1)}, s32[4,48]{1,0:T(4,128)S(1)}, u32[]{:S(2)}, u32[]{:S(2)}) collective-permute-start(s32[4,48]{1,0:T(4,128)S(1)} %pad_add_fusion.2), channel_id=1, source_target_pairs={{0,1},{1,0},{2,3},{3,2},{4,5},{5,4},{6,7},{7,6},{8,9},{9,8},{10,11... | collective-permute-start | bytes 2312 | tf_op jit(solution)/shard_map/ppermute | solution.py:507
  22.7 4.1 %collective-permute-done.9 = s32[4,48]{1,0:T(4,128)S(1)} collective-permute-done((s32[4,48]{1,0:T(4,128)S(1)}, s32[4,48]{1,0:T(4,128)S(1)}, u32[]{:S(2)}, u32[]{:S(2)}) %collective-permute-start.9) | collective-permute-done | bytes 800 | tf_op jit(solution)/shard_map/ppermute | solution.py:50
  27.6 3.4 %collective-permute-done.10 = s32[8,48]{1,0:T(8,128)S(1)} collective-permute-done((s32[8,48]{1,0:T(8,128)S(1)}, s32[8,48]{1,0:T(8,128)S(1)}, u32[]{:S(2)}, u32[]{:S(2)}) %collective-permute-start.10) | collective-permute-done | bytes 1568 | tf_op jit(solution)/shard_map/ppermute | solution.py:50
  31.6 7.4 %shard_map.56.table = s32[256]{0:T(256)S(1)} custom-call(s32[16,48]{1,0:T(8,128)} %pad_add_fusion.came, s32[2]{0:T(128)} %pad_add_fusion.5.where), custom_call_target="tpu_custom_call" | custom-call | tf_op jit(solution)/shard_map/pallas_call | solution.py:216
  39.1 15.4 %collective-permute-done.13.refs_3_ = bf16[4,128,2048]{2,1,0:T(8,128)(2,1)} collective-permute-done((bf16[4,128,2048]{2,1,0:T(8,128)(2,1)}, bf16[4,128,2048]{2,1,0:T(8,128)(2,1)}, u32[]{:S(2)}, u32[]{:S(2)}) %collective-permute-start.13) | collective-permute-done | bytes 2097184 | tf_op jit(solution)/shard_map/ppermute | solution.py:46
  54.5 3.2 %collective-permute-start.16 = (bf16[4,128,2048]{2,1,0:T(8,128)(2,1)}, bf16[4,128,2048]{2,1,0:T(8,128)(2,1)}, u32[]{:S(2)}, u32[]{:S(2)}) collective-permute-start(bf16[4,128,2048]{2,1,0:T(8,128)(2,1)} %collective-permute-done.13.refs_3_), channel_id=1, source_target_pairs={{0,24},{1,97},{2,26},{3,99},{4,28},{5,101},{6,30},{7,103},{8,0},{9... | collective-permute-start | bytes 6291464 | tf_op jit(solution)/shard_map/ppermute | solution.py:46
  57.7 7.2 %shard_map.58.refs_0_ = f32[1024,2048]{1,0:T(8,128)} custom-call(s32[256]{0:T(256)S(1)} %shard_map.56.table, bf16[8,16,2,128,128]{4,3,2,1,0:T(8,128)(2,1)} %bitcast.7, bf16[4,128,2048]{2,1,0:T(8,128)(2,1)S(1)} %shard_map.55.refs_0_, bf16[4,128,2048]{2,1,0:T(8,128)(2,1)} %shard_map.57.refs_1_, bf16[4,128,2048]{2,1,0:T(8,128)(2,1)} %collective-permute-done.12.refs_2_, ...), custom_call_target="tpu_custom_call" | custom-call | bytes 1024 | tf_op jit(solution)/shard_map/pallas_call | solution.py:468
  64.9 3.3 %shard_map.59 = (bf16[3,128,2048]{2,1,0:T(8,128)(2,1)}, bf16[3,128,2048]{2,1,0:T(8,128)(2,1)}) custom-call(s32[256]{0:T(256)S(1)} %shard_map.56.table, bf16[4,128,2048]{2,1,0:T(8,128)(2,1)S(1)} %shard_map.55.refs_0_, bf16[4,128,2048]{2,1,0:T(8,128)(2,1)} %shard_map.57.refs_1_, bf16[4,128,2048]{2,1,0:T(8,128)(2,1)} %collective-permute-done.12.refs_2_, ...), custom_call_target="tpu_custom_call" | custom-call | bytes 1024 | tf_op jit(solution)/shard_map/pallas_call | solution.py:270
  68.2 9.3 %collective-permute-done.15.refs_6_.refs_1_ = bf16[4,128,2048]{2,1,0:T(8,128)(2,1)} collective-permute-done((bf16[4,128,2048]{2,1,0:T(8,128)(2,1)}, bf16[4,128,2048]{2,1,0:T(8,128)(2,1)}, u32[]{:S(2)}, u32[]{:S(2)}) %collective-permute-start.15) | collective-permute-done | bytes 2097184 | tf_op jit(solution)/shard_map/ppermute | solution.py:46
  78.4 1.8 collective-permute-start.18
  81.0 3.4 %shard_map.60 = (bf16[3,128,2048]{2,1,0:T(8,128)(2,1)}, bf16[3,128,2048]{2,1,0:T(8,128)(2,1)}) custom-call(s32[256]{0:T(256)S(1)} %shard_map.56.table, bf16[4,128,2048]{2,1,0:T(8,128)(2,1)S(1)} %shard_map.55.refs_0_, bf16[4,128,2048]{2,1,0:T(8,128)(2,1)} %shard_map.57.refs_1_, bf16[4,128,2048]{2,1,0:T(8,128)(2,1)} %collective-permute-done.12.refs_2_, ...), custom_call_target="tpu_custom_call" | custom-call | bytes 1024 | tf_op jit(solution)/shard_map/pallas_call | solution.py:270
  85.4 1.7 collective-permute-start.20
  87.1 11.5 %collective-permute-done.17.refs_8_.refs_3_ = bf16[3,128,2048]{2,1,0:T(8,128)(2,1)} collective-permute-done((bf16[3,128,2048]{2,1,0:T(8,128)(2,1)}, bf16[3,128,2048]{2,1,0:T(8,128)(2,1)}, u32[]{:S(2)}, u32[]{:S(2)}) %collective-permute-start.17) | collective-permute-done | bytes 1572896 | tf_op jit(solution)/shard_map/ppermute | solution.py:50
  99.7 4.0 %shard_map.63 = (bf16[3,128,2048]{2,1,0:T(8,128)(2,1)}, bf16[3,128,2048]{2,1,0:T(8,128)(2,1)}) custom-call(s32[256]{0:T(256)S(1)} %shard_map.56.table, bf16[4,128,2048]{2,1,0:T(8,128)(2,1)S(1)} %shard_map.55.refs_0_, bf16[4,128,2048]{2,1,0:T(8,128)(2,1)} %shard_map.57.refs_1_, bf16[4,128,2048]{2,1,0:T(8,128)(2,1)} %collective-permute-done.12.refs_2_, ...), custom_call_target="tpu_custom_call" | custom-call | bytes 1024 | tf_op jit(solution)/shard_map/pallas_call | solution.py:270
  104.0 2.8 %collective-permute-start.22 = (bf16[3,128,2048]{2,1,0:T(8,128)(2,1)}, bf16[3,128,2048]{2,1,0:T(8,128)(2,1)}, u32[]{:S(2)}, u32[]{:S(2)}) collective-permute-start(bf16[3,128,2048]{2,1,0:T(8,128)(2,1)} %get-tuple-element.214), channel_id=1, source_target_pairs={{0,96},{1,25},{2,98},{3,27},{4,100},{5,29},{6,102},{7,31},{8,104},... | collective-permute-start | bytes 4718600 | tf_op jit(solution)/shard_map/ppermute | solution.py:50
  106.8 8.7 %collective-permute-done.19.refs_10_.refs_5_ = bf16[3,128,2048]{2,1,0:T(8,128)(2,1)} collective-permute-done((bf16[3,128,2048]{2,1,0:T(8,128)(2,1)}, bf16[3,128,2048]{2,1,0:T(8,128)(2,1)}, u32[]{:S(2)}, u32[]{:S(2)}) %collective-permute-start.19) | collective-permute-done | bytes 1572896 | tf_op jit(solution)/shard_map/ppermute | solution.py:50
  116.6 3.4 %shard_map.61 = (bf16[3,128,2048]{2,1,0:T(8,128)(2,1)}, bf16[3,128,2048]{2,1,0:T(8,128)(2,1)}) custom-call(s32[256]{0:T(256)S(1)} %shard_map.56.table, bf16[4,128,2048]{2,1,0:T(8,128)(2,1)S(1)} %shard_map.55.refs_0_, bf16[4,128,2048]{2,1,0:T(8,128)(2,1)} %shard_map.57.refs_1_, bf16[4,128,2048]{2,1,0:T(8,128)(2,1)} %collective-permute-done.12.refs_2_, ...), custom_call_target="tpu_custom_call" | custom-call | bytes 1024 | tf_op jit(solution)/shard_map/pallas_call | solution.py:270
  120.8 2.8 %collective-permute-start.24 = (bf16[3,128,2048]{2,1,0:T(8,128)(2,1)}, bf16[3,128,2048]{2,1,0:T(8,128)(2,1)}, u32[]{:S(2)}, u32[]{:S(2)}) collective-permute-start(bf16[3,128,2048]{2,1,0:T(8,128)(2,1)} %get-tuple-element.218), channel_id=1, source_target_pairs={{0,96},{1,25},{2,98},{3,27},{4,100},{5,29},{6,102},{7,31},{8,104},... | collective-permute-start | bytes 4718600 | tf_op jit(solution)/shard_map/ppermute | solution.py:50
  125.4 10.6 %shard_map.62.refs_0_ = f32[1024,2048]{1,0:T(8,128)} custom-call(s32[256]{0:T(256)S(1)} %shard_map.56.table, bf16[8,16,2,128,128]{4,3,2,1,0:T(8,128)(2,1)} %bitcast.8, f32[1024,2048]{1,0:T(8,128)} %shard_map.58.refs_0_, bf16[4,128,2048]{2,1,0:T(8,128)(2,1)} %collective-permute-done.15.refs_6_.refs_1_, ...), custom_call_target="tpu_custom_call" | custom-call | bytes 1024 | tf_op jit(solution)/shard_map/pallas_call | solution.py:468
  136.0 8.0 %shard_map.64 = f32[1024,2048]{1,0:T(8,128)} custom-call(s32[256]{0:T(256)S(1)} %shard_map.56.table, bf16[8,16,2,128,128]{4,3,2,1,0:T(8,128)(2,1)} %bitcast.9, f32[1024,2048]{1,0:T(8,128)} %shard_map.62.refs_0_, bf16[3,128,2048]{2,1,0:T(8,128)(2,1)} %collective-permute-done.21.refs_1_, bf16[3,128,2048]{2,1,0:T(8,128)(2,1)} %collective-permute-done.22.refs_2_), custom_call_target="tpu_custom_call" | custom-call | bytes 1024 | tf_op jit(solution)/shard_map/pallas_call | solution.py:468
  144.0 5.2 %collective-permute-done.23 = bf16[3,128,2048]{2,1,0:T(8,128)(2,1)} collective-permute-done((bf16[3,128,2048]{2,1,0:T(8,128)(2,1)}, bf16[3,128,2048]{2,1,0:T(8,128)(2,1)}, u32[]{:S(2)}, u32[]{:S(2)}) %collective-permute-start.23) | collective-permute-done | bytes 1572896 | tf_op jit(solution)/shard_map/ppermute | solution.py:50
  150.3 9.4 %conditional.1 = (f32[16,16]{1,0:T(8,128)S(1)}) conditional(s32[]{:T(128)} %bitcast.2, (s32[256]{0:T(256)S(1)}, bf16[8,16,2,128,128]{4,3,2,1,0:T(8,128)(2,1)}, f32[1024,2048]{1,0:T(8,128)}, bf16[256,256]{1,0:T(8,128)(2,1)S(1)}, bf16[4,128,2048]{2,1,0:T(8,128)(2,1)S(1)}, /*index=5*/bf16[4,128,2048]{2,1,0:T(8,128)(2,1)}, ...), branch_computations={%region_0.0_spmd, %region_1.0_spmd, %region_2.0_spmd} | conditional | bytes 37752032 | solution.py:562
  150.3 9.2 %branch_0_fun.1 = f32[16,16]{1,0:T(8,128)S(1)} custom-call(s32[256]{0:T(256)S(1)} %get-tuple-element.104.table, bf16[8,16,2,128,128]{4,3,2,1,0:T(8,128)(2,1)} %get-tuple-element.106.own_c, f32[1024,2048]{1,0:T(8,128)} %get-tuple-element.107.before, bf16[256,256]{1,0:T(8,128)(2,1)S(1)} %get-tuple-element.108.turn, ...), custom_call_target="tpu_custom_call" | custom-call | bytes 1024 | tf_op jit(solution)/shard_map/cond/branch_0_fun/pallas_call | solution.py:468
  159.8 20.9 %all_to_all.9 = f32[128,1,2]{2,1,0:T(1,128)S(1)} all-to-all(f32[128,1,2]{2,1,0:T(1,128)S(1)} %bitcast.13), channel_id=1, replica_groups=mesh['ao'=16,'aux'=8] {'ao','aux'}, dimensions={0} | all-to-all | bytes 2048 | tf_op jit(solution)/shard_map/all_to_all | solution.py:564
  (37 shorter events, 11.0 us)
Async XLA Ops:
  0.0 2.6 %copy-start.5 = (s32[1,16,2]{1,2,0:T(2,128)S(1)}, s32[1,16,2]{1,2,0:T(2,128)}, u32[]{:S(2)}) copy-start(s32[1,16,2]{1,2,0:T(2,128)} %param.9) | copy-start | bytes 388
  0.0 2.8 %copy-start.6 = (s32[1,16]{1,0:T(1,128)S(1)}, s32[1,16]{1,0:T(1,128)}, u32[]{:S(2)}) copy-start(s32[1,16]{1,0:T(1,128)} %param.10) | copy-start | bytes 196
  2.8 5.8 %collective-permute-start.6 = (s32[1,48]{1,0:T(1,128)S(1)}, s32[1,48]{1,0:T(1,128)S(1)}, u32[]{:S(2)}, u32[]{:S(2)}) collective-permute-start(s32[1,48]{1,0:T(1,128)S(1)} %pad_add_fusion.4), channel_id=1, source_target_pairs={{0,32},{1,9},{2,34},{3,11},{4,36},{5,13},{6,38},{7,15},{8,40},{9,1... | collective-permute-start | bytes 584 | tf_op jit(solution)/shard_map/ppermute | solution.py:50
  4.9 34.1 %collective-permute-start.11 = (bf16[4,128,2048]{2,1,0:T(8,128)(2,1)S(1)}, bf16[4,128,2048]{2,1,0:T(8,128)(2,1)}, u32[]{:S(2)}, u32[]{:S(2)}) collective-permute-start(bf16[4,128,2048]{2,1,0:T(8,128)(2,1)S(1)} %shard_map.55.refs_0_), channel_id=1, source_target_pairs={{0,8},{1,33},{2,10},{3,35},{4,12},{5,37},{6,14},{7,39},{8,16},{9,4... | collective-permute-start | bytes 6291464 | tf_op jit(solution)/shard_map/ppermute | solution.py:46
  6.5 32.5 %collective-permute-start.12 = (bf16[4,128,2048]{2,1,0:T(8,128)(2,1)S(1)}, bf16[4,128,2048]{2,1,0:T(8,128)(2,1)}, u32[]{:S(2)}, u32[]{:S(2)}) collective-permute-start(bf16[4,128,2048]{2,1,0:T(8,128)(2,1)S(1)} %shard_map.55.refs_0_), channel_id=1, source_target_pairs={{0,24},{1,97},{2,26},{3,99},{4,28},{5,101},{6,30},{7,103},{8,0},{9... | collective-permute-start | bytes 6291464 | tf_op jit(solution)/shard_map/ppermute | solution.py:46
  12.6 41.9 %collective-permute-start.13 = (bf16[4,128,2048]{2,1,0:T(8,128)(2,1)}, bf16[4,128,2048]{2,1,0:T(8,128)(2,1)}, u32[]{:S(2)}, u32[]{:S(2)}) collective-permute-start(bf16[4,128,2048]{2,1,0:T(8,128)(2,1)} %shard_map.57.refs_1_), channel_id=1, source_target_pairs={{0,24},{1,97},{2,26},{3,99},{4,28},{5,101},{6,30},{7,103},{8,0},{9... | collective-permute-start | bytes 6291464 | tf_op jit(solution)/shard_map/ppermute | solution.py:46
  15.0 4.0 %collective-permute-start.7 = (s32[2,48]{1,0:T(2,128)S(1)}, s32[2,48]{1,0:T(2,128)S(1)}, u32[]{:S(2)}, u32[]{:S(2)}) collective-permute-start(s32[2,48]{1,0:T(2,128)S(1)} %pad_add_fusion.3), channel_id=1, source_target_pairs={{0,64},{1,17},{2,66},{3,19},{4,68},{5,21},{6,70},{7,23},{8,72},{9,... | collective-permute-start | bytes 1160 | tf_op jit(solution)/shard_map/ppermute | solution.py:50
  19.0 3.7 %collective-permute-start.8 = (s32[4,48]{1,0:T(4,128)S(1)}, s32[4,48]{1,0:T(4,128)S(1)}, u32[]{:S(2)}, u32[]{:S(2)}) collective-permute-start(s32[4,48]{1,0:T(4,128)S(1)} %pad_add_fusion.2), channel_id=1, source_target_pairs={{0,1},{1,0},{2,3},{3,2},{4,5},{5,4},{6,7},{7,6},{8,9},{9,8},{10,11... | collective-permute-start | bytes 2312 | tf_op jit(solution)/shard_map/ppermute | solution.py:507
  22.7 4.1 %collective-permute-start.9 = (s32[4,48]{1,0:T(4,128)S(1)}, s32[4,48]{1,0:T(4,128)S(1)}, u32[]{:S(2)}, u32[]{:S(2)}) collective-permute-start(s32[4,48]{1,0:T(4,128)S(1)} %collective-permute-done.8), channel_id=1, source_target_pairs={{0,32},{1,9},{2,34},{3,11},{4,36},{5,13},{6,38},{7,15},{8,40},{9,1... | collective-permute-start | bytes 2312 | tf_op jit(solution)/shard_map/ppermute | solution.py:50
  26.8 4.1 %collective-permute-start.10 = (s32[8,48]{1,0:T(8,128)S(1)}, s32[8,48]{1,0:T(8,128)S(1)}, u32[]{:S(2)}, u32[]{:S(2)}) collective-permute-start(s32[8,48]{1,0:T(8,128)S(1)} %pad_add_fusion.1), channel_id=1, source_target_pairs={{0,64},{1,17},{2,66},{3,19},{4,68},{5,21},{6,70},{7,23},{8,72},{9,... | collective-permute-start | bytes 4616 | tf_op jit(solution)/shard_map/ppermute | solution.py:50
  27.6 30.1 %collective-permute-start.14 = (bf16[4,128,2048]{2,1,0:T(8,128)(2,1)}, bf16[4,128,2048]{2,1,0:T(8,128)(2,1)}, u32[]{:S(2)}, u32[]{:S(2)}) collective-permute-start(bf16[4,128,2048]{2,1,0:T(8,128)(2,1)} %shard_map.57.refs_1_), channel_id=1, source_target_pairs={{0,8},{1,33},{2,10},{3,35},{4,12},{5,37},{6,14},{7,39},{8,16},{9,4... | collective-permute-start | bytes 6291464 | tf_op jit(solution)/shard_map/ppermute | solution.py:46
  39.0 38.5 %collective-permute-start.15 = (bf16[4,128,2048]{2,1,0:T(8,128)(2,1)}, bf16[4,128,2048]{2,1,0:T(8,128)(2,1)}, u32[]{:S(2)}, u32[]{:S(2)}) collective-permute-start(bf16[4,128,2048]{2,1,0:T(8,128)(2,1)} %collective-permute-done.11.refs_4_), channel_id=1, source_target_pairs={{0,8},{1,33},{2,10},{3,35},{4,12},{5,37},{6,14},{7,39},{8,16},{9,4... | collective-permute-start | bytes 6291464 | tf_op jit(solution)/shard_map/ppermute | solution.py:46
  54.5 26.5 %collective-permute-start.16 = (bf16[4,128,2048]{2,1,0:T(8,128)(2,1)}, bf16[4,128,2048]{2,1,0:T(8,128)(2,1)}, u32[]{:S(2)}, u32[]{:S(2)}) collective-permute-start(bf16[4,128,2048]{2,1,0:T(8,128)(2,1)} %collective-permute-done.13.refs_3_), channel_id=1, source_target_pairs={{0,24},{1,97},{2,26},{3,99},{4,28},{5,101},{6,30},{7,103},{8,0},{9... | collective-permute-start | bytes 6291464 | tf_op jit(solution)/shard_map/ppermute | solution.py:46
  77.5 21.1 %collective-permute-start.17 = (bf16[3,128,2048]{2,1,0:T(8,128)(2,1)}, bf16[3,128,2048]{2,1,0:T(8,128)(2,1)}, u32[]{:S(2)}, u32[]{:S(2)}) collective-permute-start(bf16[3,128,2048]{2,1,0:T(8,128)(2,1)} %get-tuple-element.201), channel_id=1, source_target_pairs={{0,32},{1,9},{2,34},{3,11},{4,36},{5,13},{6,38},{7,15},{8,40},{9,1... | collective-permute-start | bytes 4718600 | tf_op jit(solution)/shard_map/ppermute | solution.py:50
  78.4 21.3 %collective-permute-start.18 = (bf16[3,128,2048]{2,1,0:T(8,128)(2,1)}, bf16[3,128,2048]{2,1,0:T(8,128)(2,1)}, u32[]{:S(2)}, u32[]{:S(2)}) collective-permute-start(bf16[3,128,2048]{2,1,0:T(8,128)(2,1)} %get-tuple-element.202), channel_id=1, source_target_pairs={{0,96},{1,25},{2,98},{3,27},{4,100},{5,29},{6,102},{7,31},{8,104},... | collective-permute-start | bytes 4718600 | tf_op jit(solution)/shard_map/ppermute | solution.py:50
  84.4 31.1 %collective-permute-start.19 = (bf16[3,128,2048]{2,1,0:T(8,128)(2,1)}, bf16[3,128,2048]{2,1,0:T(8,128)(2,1)}, u32[]{:S(2)}, u32[]{:S(2)}) collective-permute-start(bf16[3,128,2048]{2,1,0:T(8,128)(2,1)} %get-tuple-element.205), channel_id=1, source_target_pairs={{0,32},{1,9},{2,34},{3,11},{4,36},{5,13},{6,38},{7,15},{8,40},{9,1... | collective-permute-start | bytes 4718600 | tf_op jit(solution)/shard_map/ppermute | solution.py:50
  85.4 31.2 %collective-permute-start.20 = (bf16[3,128,2048]{2,1,0:T(8,128)(2,1)}, bf16[3,128,2048]{2,1,0:T(8,128)(2,1)}, u32[]{:S(2)}, u32[]{:S(2)}) collective-permute-start(bf16[3,128,2048]{2,1,0:T(8,128)(2,1)} %get-tuple-element.206), channel_id=1, source_target_pairs={{0,96},{1,25},{2,98},{3,27},{4,100},{5,29},{6,102},{7,31},{8,104},... | collective-permute-start | bytes 4718600 | tf_op jit(solution)/shard_map/ppermute | solution.py:50
  103.7 32.2 %collective-permute-start.21 = (bf16[3,128,2048]{2,1,0:T(8,128)(2,1)}, bf16[3,128,2048]{2,1,0:T(8,128)(2,1)}, u32[]{:S(2)}, u32[]{:S(2)}) collective-permute-start(bf16[3,128,2048]{2,1,0:T(8,128)(2,1)} %get-tuple-element.213), channel_id=1, source_target_pairs={{0,32},{1,9},{2,34},{3,11},{4,36},{5,13},{6,38},{7,15},{8,40},{9,1... | collective-permute-start | bytes 4718600 | tf_op jit(solution)/shard_map/ppermute | solution.py:50
  104.0 19.5 %copy-start.4 = (bf16[1,128,128]{2,1,0:T(8,128)(2,1)S(1)}, bf16[1,128,128]{2,1,0:T(8,128)(2,1)}, u32[]{:S(2)}) copy-start(bf16[1,128,128]{2,1,0:T(8,128)(2,1)} %param.12) | copy-start | bytes 98308
  104.0 32.0 %collective-permute-start.22 = (bf16[3,128,2048]{2,1,0:T(8,128)(2,1)}, bf16[3,128,2048]{2,1,0:T(8,128)(2,1)}, u32[]{:S(2)}, u32[]{:S(2)}) collective-permute-start(bf16[3,128,2048]{2,1,0:T(8,128)(2,1)} %get-tuple-element.214), channel_id=1, source_target_pairs={{0,96},{1,25},{2,98},{3,27},{4,100},{5,29},{6,102},{7,31},{8,104},... | collective-permute-start | bytes 4718600 | tf_op jit(solution)/shard_map/ppermute | solution.py:50
  120.0 29.2 %collective-permute-start.23 = (bf16[3,128,2048]{2,1,0:T(8,128)(2,1)}, bf16[3,128,2048]{2,1,0:T(8,128)(2,1)}, u32[]{:S(2)}, u32[]{:S(2)}) collective-permute-start(bf16[3,128,2048]{2,1,0:T(8,128)(2,1)} %get-tuple-element.217), channel_id=1, source_target_pairs={{0,32},{1,9},{2,34},{3,11},{4,36},{5,13},{6,38},{7,15},{8,40},{9,1... | collective-permute-start | bytes 4718600 | tf_op jit(solution)/shard_map/ppermute | solution.py:50
  120.8 29.5 %collective-permute-start.24 = (bf16[3,128,2048]{2,1,0:T(8,128)(2,1)}, bf16[3,128,2048]{2,1,0:T(8,128)(2,1)}, u32[]{:S(2)}, u32[]{:S(2)}) collective-permute-start(bf16[3,128,2048]{2,1,0:T(8,128)(2,1)} %get-tuple-element.218), channel_id=1, source_target_pairs={{0,96},{1,25},{2,98},{3,27},{4,100},{5,29},{6,102},{7,31},{8,104},... | collective-permute-start | bytes 4718600 | tf_op jit(solution)/shard_map/ppermute | solution.py:50
